TPU v7x, 32 devices: a whole 2x2x4 slice. The times are simulated.
32 devices in a mesh: section: 2 (over x), dp: 8 (over z, y), tensor: 2 (over core).
Axes of the slice: x: 2, y: 2, z: 4, core: 2. Of those that a mesh axis runs over, the one named last changes fastest.
Arguments:
- frames: bfloat16 [4, 1024, 1024], P(None, 'dp'), may hold values from -6 to 6
- codes: int32 [4, 1024, 3], P(None, 'dp'), may hold values from 0 to 1023
- lengths: int32 [4, 16], replicated, may hold values from 0 to 1024, as said below
- gains: float32 [2, 2, 1024], P('section'), may hold values from 0.5 to 1.5
- w_qkv: bfloat16 [2, 1024, 3, 1024], P('section', None, None, 'tensor'), may hold values from -0.1875 to 0.1875
- w_out: bfloat16 [2, 1024, 1024], P('section', 'tensor'), may hold values from -0.5 to 0.5
- w_up: bfloat16 [2, 1024, 4096], P('section', None, 'tensor'), may hold values from -0.1875 to 0.1875
- w_down: bfloat16 [2, 4096, 1024], P('section', 'tensor'), may hold values from -0.09375 to 0.09375
- table: bfloat16 [3, 1024, 1024], replicated, may hold values from -6 to 6
- cotangent: bfloat16 [4, 1024, 3, 1024], P(None, 'dp'), may hold values from -6 to 6
Outputs:
- global_out: bfloat16 [4, 1024, 1024], P(None, 'dp')
- local_out: bfloat16 [4, 1024, 3, 1024], P(None, 'dp')
- input_grads: float32 [2, 4, 1024, 1024], P('section', None, 'dp')
- grad_qkv: float32 [2, 1024, 3, 1024], P('section', 'dp', None, 'tensor')
- grad_out: float32 [2, 1024, 1024], P('section', 'tensor', 'dp')
- grad_up: float32 [2, 1024, 4096], P('section', 'dp', 'tensor')
- grad_down: float32 [2, 4096, 1024], P('section', 'tensor', 'dp')
- grad_gains: float32 [2, 2, 1024], P('section', None, 'dp')
- grad_table: float32 [3, 1024, 1024], P(None, ('section', 'dp'))
Inputs may be any that keep to these rules, and one draw needn't show every extreme that they name: In every draw one micro-batch, drawn from the seed, holds a single sequence of 1024 frames; in the others the lengths add up to less than 1024 and the frames after the last sequence are padding. A slot of length 0 is unused.
All inputs are finite; a program needn't handle non-finite values.
Results may differ from a plain program's by a relative error of at most 0.015.
Values may be sent and summed in bfloat16 or wider, within the bound.
No kernel may reach another device: no remote copies, remote signals or barrier semaphores. Data moves between devices by JAX's collectives and lax.ppermute only.
A program may use at most 256 MiB of HBM per device.

v0:
```python
import jax
import jax.numpy as jnp
from jax import lax
from jax.sharding import PartitionSpec as P

HEAD = 64
CODEBOOKS = 3


eps = 1e-05
far = -1e30


def from_behind(block, axis, distance):
    devices = range(lax.axis_size(axis))
    route = [(i - distance, i) for i in devices if i - distance in devices]
    return lax.ppermute(block, axis, route)


def rms_scale(values):
    return lax.rsqrt(jnp.mean(values * values, axis=-1, keepdims=True) + eps)


def rms_back(values, gain_row, grad_normed):
    factor = rms_scale(values)
    normal = values * factor
    grad_unit = grad_normed * gain_row
    grad_values = factor * (
        grad_unit - normal * jnp.mean(grad_unit * normal, axis=-1, keepdims=True)
    )
    return (grad_values, jnp.sum(grad_normed * normal, axis=0))


def head_total(partial_sum):
    return lax.psum(partial_sum, "tensor")


def matmul(left, right):
    return jnp.dot(left, right, preferred_element_type=jnp.float32)


def across_rows(left, right):
    return lax.dot_general(
        left, right, (((0,), (0,)), ((), ())), preferred_element_type=jnp.float32
    )


def against_rows(left, right):
    return lax.dot_general(
        left, right, (((1,), (1,)), ((), ())), preferred_element_type=jnp.float32
    )


def smooth_gate(values):
    return jax.nn.gelu(values, approximate=True)


def doc_index(positions, doc_ends):
    return jnp.sum((positions[:, None] >= doc_ends[None, :]).astype(jnp.int32), axis=1)


def allowed_mask(query_pos, key_pos, doc_ends):
    same_doc = doc_index(query_pos, doc_ends)[:, None] == doc_index(key_pos, doc_ends)[None, :]
    earlier = key_pos[None, :] <= query_pos[:, None]
    live = (key_pos < doc_ends[-1])[None, :]
    return same_doc & earlier & live | (key_pos[None, :] == query_pos[:, None])


def masked_softmax(scores, mask, factor):
    logits = jnp.where(mask, scores * factor, far)
    top = jnp.max(logits, axis=-1, keepdims=True)
    weights = jnp.exp(logits - top)
    mass = jnp.sum(weights, axis=-1, keepdims=True)
    return (weights / mass, (top + jnp.log(mass))[..., 0])


def frame_forward(packed, query_pos, doc_ends, head_count):
    row_count = packed.shape[0]
    width = packed.shape[1] // 3
    factor = HEAD ** (-0.5)
    parts = packed.reshape(row_count, 3, width)
    all_keys, all_values = (
        lax.all_gather(parts[:, 1], "dp", axis=0, tiled=True),
        lax.all_gather(parts[:, 2], "dp", axis=0, tiled=True),
    )
    key_count = all_keys.shape[0]
    key_pos = jnp.arange(key_count, dtype=jnp.int32)
    mask = allowed_mask(query_pos, key_pos, doc_ends)
    queries = parts[:, 0].reshape(row_count, head_count, -1)
    scores = jnp.einsum(
        "qhe,khe->hqk",
        queries,
        all_keys.reshape(key_count, head_count, -1),
        preferred_element_type=jnp.float32,
    )
    probs, log_mass = masked_softmax(scores, mask[None], factor)
    attended = jnp.einsum(
        "hqk,khe->qhe",
        probs.astype(jnp.bfloat16),
        all_values.reshape(key_count, head_count, -1),
        preferred_element_type=jnp.float32,
    )
    return (attended.reshape(row_count, width), log_mass)


def frame_backward(packed, grad_att, log_mass, query_pos, doc_ends, head_count):
    row_count = packed.shape[0]
    width = packed.shape[1] // 3
    factor = HEAD ** (-0.5)
    parts = packed.reshape(row_count, 3, width)
    all_keys, all_values = (
        lax.all_gather(parts[:, 1], "dp", axis=0, tiled=True),
        lax.all_gather(parts[:, 2], "dp", axis=0, tiled=True),
    )
    key_count = all_keys.shape[0]
    key_pos = jnp.arange(key_count, dtype=jnp.int32)
    queries = parts[:, 0].reshape(row_count, head_count, -1)
    grad_heads = grad_att.reshape(row_count, head_count, -1)
    keys_heads = all_keys.reshape(key_count, head_count, -1)
    scores = jnp.einsum("qhe,khe->hqk", queries, keys_heads, preferred_element_type=jnp.float32)
    mask = allowed_mask(query_pos, key_pos, doc_ends)
    probs = jnp.exp(jnp.where(mask[None], scores * factor, far) - log_mass[:, :, None])
    grad_probs = jnp.einsum(
        "qhe,khe->hqk",
        grad_heads,
        all_values.reshape(key_count, head_count, -1),
        preferred_element_type=jnp.float32,
    )
    spread = jnp.sum(probs * grad_probs, axis=-1)
    grad_scores = (probs * (grad_probs - spread[:, :, None]) * factor).astype(jnp.bfloat16)
    grad_queries = jnp.einsum(
        "hqk,khe->qhe", grad_scores, keys_heads, preferred_element_type=jnp.float32
    ).reshape(row_count, width)
    keys_term = jnp.einsum(
        "hqk,qhe->khe", grad_scores, queries, preferred_element_type=jnp.float32
    ).reshape(key_count, width)
    values_term = jnp.einsum(
        "hqk,qhe->khe", probs.astype(jnp.bfloat16), grad_heads, preferred_element_type=jnp.float32
    ).reshape(key_count, width)
    grad_keys, grad_values = (
        lax.psum_scatter(keys_term, "dp", scatter_dimension=0, tiled=True),
        lax.psum_scatter(values_term, "dp", scatter_dimension=0, tiled=True),
    )
    return jnp.stack([grad_queries, grad_keys, grad_values], axis=1).reshape(row_count, 3 * width)


def codebook_forward(packed, head_count):
    row_count = packed.shape[0]
    width = packed.shape[1] // 3
    factor = HEAD ** (-0.5)
    parts = packed.reshape(row_count // CODEBOOKS, CODEBOOKS, 3, head_count, -1)
    scores = jnp.einsum(
        "nche,ndhe->nhcd", parts[:, :, 0], parts[:, :, 1], preferred_element_type=jnp.float32
    )
    order = jnp.arange(CODEBOOKS, dtype=jnp.int32)
    mask = order[None, :] <= order[:, None]
    probs, log_mass = masked_softmax(scores, mask, factor)
    attended = jnp.einsum(
        "nhcd,ndhe->nche",
        probs.astype(jnp.bfloat16),
        parts[:, :, 2],
        preferred_element_type=jnp.float32,
    )
    return (attended.reshape(row_count, width), probs)


def codebook_backward(packed, grad_att, probs, head_count):
    row_count = packed.shape[0]
    width = packed.shape[1] // 3
    factor = HEAD ** (-0.5)
    parts = packed.reshape(row_count // CODEBOOKS, CODEBOOKS, 3, head_count, -1)
    grad_heads = grad_att.reshape(row_count // CODEBOOKS, CODEBOOKS, head_count, -1)
    grad_probs = jnp.einsum(
        "nche,ndhe->nhcd", grad_heads, parts[:, :, 2], preferred_element_type=jnp.float32
    )
    spread = jnp.sum(probs * grad_probs, axis=-1, keepdims=True)
    grad_scores = (probs * (grad_probs - spread) * factor).astype(jnp.bfloat16)
    grad_queries = jnp.einsum(
        "nhcd,ndhe->nche", grad_scores, parts[:, :, 1], preferred_element_type=jnp.float32
    )
    grad_keys = jnp.einsum(
        "nhcd,nche->ndhe", grad_scores, parts[:, :, 0], preferred_element_type=jnp.float32
    )
    grad_values = jnp.einsum(
        "nhcd,nche->ndhe",
        probs.astype(jnp.bfloat16),
        grad_heads,
        preferred_element_type=jnp.float32,
    )
    return jnp.stack([grad_queries, grad_keys, grad_values], axis=2).reshape(row_count, 3 * width)


def layer_forward(inputs, gain_pair, layer_weights, attend):
    w_proj, w_mix, w_rise, w_fall = layer_weights
    normed = (inputs * rms_scale(inputs) * gain_pair[0]).astype(jnp.bfloat16)
    packed = matmul(normed, w_proj.reshape(w_proj.shape[0], -1)).astype(jnp.bfloat16)
    attended, saved = attend(packed)
    attended_low = attended.astype(jnp.bfloat16)
    resid = inputs + head_total(matmul(attended_low, w_mix))
    normed_mid = (resid * rms_scale(resid) * gain_pair[1]).astype(jnp.bfloat16)
    rise = matmul(normed_mid, w_rise)
    active = smooth_gate(rise).astype(jnp.bfloat16)
    result = resid + head_total(matmul(active, w_fall))
    return (result, (normed, packed, attended_low, saved, resid, normed_mid, rise, active))


def layer_backward(inputs, gain_pair, layer_weights, kept, grad_result, attend_back):
    w_proj, w_mix, w_rise, w_fall = layer_weights
    normed, packed, attended_low, saved, resid, normed_mid, rise, active = kept
    grad_fall_low = grad_result.astype(jnp.bfloat16)
    grad_fall_w = across_rows(active, grad_fall_low)
    grad_active = against_rows(grad_fall_low, w_fall)
    grad_rise = jax.vjp(smooth_gate, rise)[1](grad_active)[0].astype(jnp.bfloat16)
    grad_rise_w = across_rows(normed_mid, grad_rise)
    grad_mid = head_total(against_rows(grad_rise, w_rise))
    back_mid, gain_mid = rms_back(resid, gain_pair[1], grad_mid)
    grad_resid = grad_result + back_mid
    resid_low = grad_resid.astype(jnp.bfloat16)
    grad_mix_w = across_rows(attended_low, resid_low)
    grad_att = against_rows(resid_low, w_mix).astype(jnp.bfloat16)
    grad_packed = attend_back(packed, grad_att, saved).astype(jnp.bfloat16)
    flat_proj = w_proj.reshape(w_proj.shape[0], -1)
    grad_proj_w = across_rows(normed, grad_packed).reshape(w_proj.shape)
    grad_normed = head_total(against_rows(grad_packed, flat_proj))
    back_in, gain_in = rms_back(inputs, gain_pair[0], grad_normed)
    return (
        grad_resid + back_in,
        (grad_proj_w, grad_mix_w, grad_rise_w, grad_fall_w, jnp.stack([gain_in, gain_mid])),
    )


def body(frames, codes, lengths, gains, w_qkv, w_out, w_up, w_down, table, cotangent):
    on_first = lax.axis_index("section") == 0
    head_count = w_qkv.shape[3] // HEAD
    layer_weights = (w_qkv[0], w_out[0], w_up[0], w_down[0])
    gains_here = gains[0]
    frame_count = frames.shape[1]
    query_pos = lax.axis_index("dp") * frame_count + jnp.arange(frame_count, dtype=jnp.int32)
    zero_grads = (
        jnp.zeros(w_qkv.shape[1:], jnp.float32),
        jnp.zeros(w_out.shape[1:], jnp.float32),
        jnp.zeros(w_up.shape[1:], jnp.float32),
        jnp.zeros(w_down.shape[1:], jnp.float32),
        jnp.zeros(gains.shape[1:], jnp.float32),
    )

    def global_forward_rows(frame_rows, slot_lengths):
        doc_ends = jnp.cumsum(slot_lengths)
        return (
            doc_ends,
            layer_forward(
                frame_rows.astype(jnp.float32),
                gains_here,
                layer_weights,
                lambda packed: frame_forward(packed, query_pos, doc_ends, head_count),
            ),
        )

    def global_step(carry, inputs):
        doc_ends, (result, kept) = global_forward_rows(inputs[0], inputs[1])
        return (carry, result.astype(jnp.bfloat16))

    global_low = lax.scan(global_step, jnp.zeros((), jnp.int32), (frames, lengths))[1]
    arrived = from_behind(global_low, "section", 1)
    books = jnp.arange(CODEBOOKS, dtype=jnp.int32)
    looked_up = table[books[None, None, :], codes]
    local_in = arrived.astype(jnp.float32)[:, :, None, :] + looked_up.astype(jnp.float32)
    local_rows = local_in.reshape(-1, local_in.shape[-1])
    local_result, local_kept = layer_forward(
        local_rows, gains_here, layer_weights, lambda packed: codebook_forward(packed, head_count)
    )
    grad_rows, local_grads = layer_backward(
        local_rows,
        gains_here,
        layer_weights,
        local_kept,
        cotangent.astype(jnp.float32).reshape(local_rows.shape),
        lambda packed, grad_att, saved: codebook_backward(packed, grad_att, saved, head_count),
    )
    grad_frame = jnp.sum(grad_rows.reshape(local_in.shape), axis=2)
    table_slots = (books[None, None, :] * table.shape[1] + codes).reshape(-1)
    table_term = jax.ops.segment_sum(
        grad_rows, table_slots, num_segments=table.shape[0] * table.shape[1]
    ).reshape(table.shape)
    local_low = local_result.astype(jnp.bfloat16).reshape(cotangent.shape)
    table_part = jnp.where(on_first, jnp.zeros(table.shape, jnp.float32), table_term)
    grad_frame = jnp.where(on_first, jnp.zeros(frames.shape, jnp.float32), grad_frame)
    grad_table = lax.psum_scatter(table_part, ("section", "dp"), scatter_dimension=1, tiled=True)
    grad_back, local_copy = from_behind((grad_frame.astype(jnp.bfloat16), local_low), "section", -1)

    def global_back(totals, inputs):
        frame_rows, slot_lengths, grad_low = inputs
        doc_ends, (result, kept) = global_forward_rows(frame_rows, slot_lengths)
        grad_in, grads = layer_backward(
            frame_rows.astype(jnp.float32),
            gains_here,
            layer_weights,
            kept,
            grad_low.astype(jnp.float32),
            lambda packed, grad_att, saved: frame_backward(
                packed, grad_att, saved, query_pos, doc_ends, head_count
            ),
        )
        return (jax.tree.map(jnp.add, totals, grads), grad_in)

    global_grads, grad_frames = lax.scan(global_back, zero_grads, (frames, lengths, grad_back))

    def pick(global_part, local_part):
        return jnp.where(on_first, global_part, local_part)

    proj_sum, mix_sum, rise_sum, fall_sum, gain_sum = jax.tree.map(pick, global_grads, local_grads)
    proj_share, mix_share, rise_share, fall_share, gain_share = (
        lax.psum_scatter(proj_sum, "dp", scatter_dimension=0, tiled=True),
        lax.psum_scatter(mix_sum, "dp", scatter_dimension=1, tiled=True),
        lax.psum_scatter(rise_sum, "dp", scatter_dimension=0, tiled=True),
        lax.psum_scatter(fall_sum, "dp", scatter_dimension=1, tiled=True),
        lax.psum_scatter(gain_sum, "dp", scatter_dimension=1, tiled=True),
    )
    global_out = jnp.where(on_first, global_low, arrived)
    local_out = jnp.where(on_first, local_copy, local_low)
    input_grads = jnp.where(on_first, grad_frames, grad_frame)[None]
    return (
        global_out,
        local_out,
        input_grads,
        proj_share[None],
        mix_share[None],
        rise_share[None],
        fall_share[None],
        gain_share[None],
        grad_table,
    )


def solution(mesh):
    in_specs = (
        P(None, "dp", None),
        P(None, "dp", None),
        P(),
        P("section", None, None),
        P("section", None, None, "tensor"),
        P("section", "tensor", None),
        P("section", None, "tensor"),
        P("section", "tensor", None),
        P(),
        P(None, "dp", None, None),
    )
    out_specs = (
        P(None, "dp", None),
        P(None, "dp", None, None),
        P("section", None, "dp", None),
        P("section", "dp", None, "tensor"),
        P("section", "tensor", "dp"),
        P("section", "dp", "tensor"),
        P("section", "tensor", "dp"),
        P("section", None, "dp"),
        P(None, ("section", "dp"), None),
    )
    return jax.shard_map(body, mesh=mesh, in_specs=in_specs, out_specs=out_specs, check_vma=False)
```

profile of v0, /device:TPU:3, one launch (start us, length us, event | category | flops | bytes accessed | tf_op | source)
XLA Modules:
  0.0 3171.4 jit_solution(13343301140614211297)
XLA Ops:
  11.2 560.9 %while.36 = (s32[]{:T(128)}, bf16[4,128,1024]{2,1,0:T(8,128)(2,1)}, bf16[4,128,1024]{2,1,0:T(8,128)(2,1)}, f32[2,1024]{1,0:T(2,128)S(1)}, bf16[1,1024,3,512]{1,3...) while((s32[]{:T(128)}, bf16[4,128,1024]{2,1,0:T(8,128)(2,1)}, ...), condition=%wide.region_10.11_spmd.clone.clone, body=%wide.region_0.10_spmd.clone.sunk.clone | while | flops 1891687936 | bytes 48023000 | solution.py:263
  20.6 37.2 %all-gather.27.cloned.1.call-done = bf16[1024,1,512]{0,2,1:T(8,128)(2,1)} async-done(((bf16[128,1,512]{0,2,1:T(8,128)(2,1)}), bf16[1024,1,512]{0,2,1:T(8,128)(2,1)}) %all-gather.27.cloned.1.call-update) | async-done | bytes 1048592 | tf_op jit(solution)/shard_map/while/body/eval_jaxpr/all_gather | solution.py:83
  62.6 36.4 %all-gather.25.cloned.1.call-done = bf16[1024,1,512]{0,2,1:T(8,128)(2,1)} async-done(((bf16[128,1,512]{0,2,1:T(8,128)(2,1)}), bf16[1024,1,512]{0,2,1:T(8,128)(2,1)}) %all-gather.25.cloned.1.call-update) | async-done | bytes 1048592 | tf_op jit(solution)/shard_map/while/body/eval_jaxpr/all_gather | solution.py:84
  161.3 36.6 %all-gather.27.cloned.1.call-done = bf16[1024,1,512]{0,2,1:T(8,128)(2,1)} async-done(((bf16[128,1,512]{0,2,1:T(8,128)(2,1)}), bf16[1024,1,512]{0,2,1:T(8,128)(2,1)}) %all-gather.27.cloned.1.call-update) | async-done | bytes 1048592 | tf_op jit(solution)/shard_map/while/body/eval_jaxpr/all_gather | solution.py:83
  202.8 36.3 %all-gather.25.cloned.1.call-done = bf16[1024,1,512]{0,2,1:T(8,128)(2,1)} async-done(((bf16[128,1,512]{0,2,1:T(8,128)(2,1)}), bf16[1024,1,512]{0,2,1:T(8,128)(2,1)}) %all-gather.25.cloned.1.call-update) | async-done | bytes 1048592 | tf_op jit(solution)/shard_map/while/body/eval_jaxpr/all_gather | solution.py:84
  301.3 36.6 %all-gather.27.cloned.1.call-done = bf16[1024,1,512]{0,2,1:T(8,128)(2,1)} async-done(((bf16[128,1,512]{0,2,1:T(8,128)(2,1)}), bf16[1024,1,512]{0,2,1:T(8,128)(2,1)}) %all-gather.27.cloned.1.call-update) | async-done | bytes 1048592 | tf_op jit(solution)/shard_map/while/body/eval_jaxpr/all_gather | solution.py:83
  342.8 36.3 %all-gather.25.cloned.1.call-done = bf16[1024,1,512]{0,2,1:T(8,128)(2,1)} async-done(((bf16[128,1,512]{0,2,1:T(8,128)(2,1)}), bf16[1024,1,512]{0,2,1:T(8,128)(2,1)}) %all-gather.25.cloned.1.call-update) | async-done | bytes 1048592 | tf_op jit(solution)/shard_map/while/body/eval_jaxpr/all_gather | solution.py:84
  441.3 36.6 %all-gather.27.cloned.1.call-done = bf16[1024,1,512]{0,2,1:T(8,128)(2,1)} async-done(((bf16[128,1,512]{0,2,1:T(8,128)(2,1)}), bf16[1024,1,512]{0,2,1:T(8,128)(2,1)}) %all-gather.27.cloned.1.call-update) | async-done | bytes 1048592 | tf_op jit(solution)/shard_map/while/body/eval_jaxpr/all_gather | solution.py:83
  482.7 36.3 %all-gather.25.cloned.1.call-done = bf16[1024,1,512]{0,2,1:T(8,128)(2,1)} async-done(((bf16[128,1,512]{0,2,1:T(8,128)(2,1)}), bf16[1024,1,512]{0,2,1:T(8,128)(2,1)}) %all-gather.25.cloned.1.call-update) | async-done | bytes 1048592 | tf_op jit(solution)/shard_map/while/body/eval_jaxpr/all_gather | solution.py:84
  943.2 48.7 %all-reduce.14.cloned.1.call-done = (f32[1536,1024]{1,0:T(8,128)}, f32[1536,1024]{1,0:T(8,128)}) async-done(((f32[1536,1024]{1,0:T(8,128)}, f32[1536,1024]{1,0:T(8,128)}), (f32[1536,1024]{1,0:T(8,128)}, f32[1536,1024]{1,0:T(8,128)})) %all-reduce.14.cloned.1.call-update) | async-done | bytes 12582928 | tf_op jit(solution)/shard_map/psum | solution.py:35
  1053.0 1285.1 %while.37 = (s32[]{:T(128)}, f32[1024,3,512]{2,0,1:T(8,128)}, f32[512,1024]{1,0:T(8,128)}, f32[1024,2048]{1,0:T(8,128)}, f32[2048,1024]{1,0:T(8,128)}, /*index=5...) while((s32[]{:T(128)}, f32[1024,3,512]{2,0,1:T(8,128)}, ...), condition=%wide.region_41.42_spmd.clone.clone, body=%wide.region_23.41_spmd.clone.sunk.clone | while | flops 5154141696 | bytes 239561824 | solution.py:306
  1063.1 38.1 %all-gather.31.cloned.1.call-done = bf16[1024,1,512]{0,2,1:T(8,128)(2,1)} async-done(((bf16[128,1,512]{0,2,1:T(8,128)(2,1)}), bf16[1024,1,512]{0,2,1:T(8,128)(2,1)}) %all-gather.31.cloned.1.call-update) | async-done | bytes 1048592 | tf_op jit(solution)/shard_map/while/body/eval_jaxpr/all_gather | solution.py:112
  1276.3 71.0 %reduce-scatter.25.cloned.1.call-done = f32[128,512]{0,1:T(8,128)} async-done(((f32[1024,512]{0,1:T(8,128)}), f32[128,512]{0,1:T(8,128)}) %reduce-scatter.25.cloned.1.call-update) | async-done | bytes 262160 | tf_op jit(solution)/shard_map/while/body/eval_jaxpr/reduce_scatter | solution.py:141
  1384.9 36.4 %all-gather.31.cloned.1.call-done = bf16[1024,1,512]{0,2,1:T(8,128)(2,1)} async-done(((bf16[128,1,512]{0,2,1:T(8,128)(2,1)}), bf16[1024,1,512]{0,2,1:T(8,128)(2,1)}) %all-gather.31.cloned.1.call-update) | async-done | bytes 1048592 | tf_op jit(solution)/shard_map/while/body/eval_jaxpr/all_gather | solution.py:112
  1596.7 72.1 %reduce-scatter.25.cloned.1.call-done = f32[128,512]{0,1:T(8,128)} async-done(((f32[1024,512]{0,1:T(8,128)}), f32[128,512]{0,1:T(8,128)}) %reduce-scatter.25.cloned.1.call-update) | async-done | bytes 262160 | tf_op jit(solution)/shard_map/while/body/eval_jaxpr/reduce_scatter | solution.py:141
  1706.0 36.4 %all-gather.31.cloned.1.call-done = bf16[1024,1,512]{0,2,1:T(8,128)(2,1)} async-done(((bf16[128,1,512]{0,2,1:T(8,128)(2,1)}), bf16[1024,1,512]{0,2,1:T(8,128)(2,1)}) %all-gather.31.cloned.1.call-update) | async-done | bytes 1048592 | tf_op jit(solution)/shard_map/while/body/eval_jaxpr/all_gather | solution.py:112
  1917.9 71.3 %reduce-scatter.25.cloned.1.call-done = f32[128,512]{0,1:T(8,128)} async-done(((f32[1024,512]{0,1:T(8,128)}), f32[128,512]{0,1:T(8,128)}) %reduce-scatter.25.cloned.1.call-update) | async-done | bytes 262160 | tf_op jit(solution)/shard_map/while/body/eval_jaxpr/reduce_scatter | solution.py:141
  2026.8 36.6 %all-gather.31.cloned.1.call-done = bf16[1024,1,512]{0,2,1:T(8,128)(2,1)} async-done(((bf16[128,1,512]{0,2,1:T(8,128)(2,1)}), bf16[1024,1,512]{0,2,1:T(8,128)(2,1)}) %all-gather.31.cloned.1.call-update) | async-done | bytes 1048592 | tf_op jit(solution)/shard_map/while/body/eval_jaxpr/all_gather | solution.py:112
  2238.5 71.5 %reduce-scatter.25.cloned.1.call-done = f32[128,512]{0,1:T(8,128)} async-done(((f32[1024,512]{0,1:T(8,128)}), f32[128,512]{0,1:T(8,128)}) %reduce-scatter.25.cloned.1.call-update) | async-done | bytes 262160 | tf_op jit(solution)/shard_map/while/body/eval_jaxpr/reduce_scatter | solution.py:141
  2464.8 62.6 %collective-permute-done.1 = bf16[4,128,3,1024]{3,1,2,0:T(8,128)(2,1)} collective-permute-done((bf16[4,128,3,1024]{3,1,2,0:T(8,128)(2,1)S(1)}, bf16[4,128,3,1024]{3,1,2,0:T(8,128)(2,1)}, u32[]{:S(2)}, u32[]{:S(2)}) %collective-permute-start.1) | collective-permute-done | bytes 3145760 | tf_op jit(solution)/shard_map/ppermute | solution.py:17
  2536.9 60.7 %reduce-scatter.11.cloned.1.call-done = f32[128,3,512]{2,0,1:T(8,128)} async-done(((f32[1024,3,512]{2,0,1:T(8,128)}), f32[128,3,512]{2,0,1:T(8,128)}) %reduce-scatter.11.cloned.1.call-update) | async-done | bytes 786448 | tf_op jit(solution)/shard_map/reduce_scatter | solution.py:313
  2597.6 151.3 %reduce-scatter.15.cloned.1.call-done = f32[128,2048]{1,0:T(8,128)} async-done(((f32[1024,2048]{1,0:T(8,128)}), f32[128,2048]{1,0:T(8,128)}) %reduce-scatter.15.cloned.1.call-update) | async-done | bytes 1048592 | tf_op jit(solution)/shard_map/reduce_scatter | solution.py:315
  2748.9 150.6 %reduce-scatter.17.cloned.1.call-done = f32[2048,128]{1,0:T(8,128)} async-done(((f32[2048,1024]{1,0:T(8,128)}), f32[2048,128]{1,0:T(8,128)}) %reduce-scatter.17.cloned.1.call-update) | async-done | bytes 1048592 | tf_op jit(solution)/shard_map/reduce_scatter | solution.py:316
  2899.5 264.1 %reduce-scatter.19.cloned.1.call-done = f32[3,64,1024]{2,1,0:T(8,128)} async-done(((f32[3,1024,1024]{2,1,0:T(8,128)}), f32[3,64,1024]{2,1,0:T(8,128)}) %reduce-scatter.19.cloned.1.call-update) | async-done | bytes 786448 | tf_op jit(solution)/shard_map/reduce_scatter | solution.py:288
  (714 shorter events, 1688.5 us)
Async XLA Ops:
  18.0 104.6 %all-reduce.16.cloned.1.call-start = ((), (), s32[]{:S(2)}) async-start(), calls=%async_computation.19 | async-start | bytes 1048576 | tf_op jit(solution)/shard_map/while/body/eval_jaxpr/psum | solution.py:35
  158.7 103.9 %all-reduce.16.cloned.1.call-start = ((), (), s32[]{:S(2)}) async-start(), calls=%async_computation.19 | async-start | bytes 1048576 | tf_op jit(solution)/shard_map/while/body/eval_jaxpr/psum | solution.py:35
  438.7 103.9 %all-reduce.16.cloned.1.call-start = ((), (), s32[]{:S(2)}) async-start(), calls=%async_computation.19 | async-start | bytes 1048576 | tf_op jit(solution)/shard_map/while/body/eval_jaxpr/psum | solution.py:35
  572.1 169.7 %all-reduce.10.cloned.1.call-start = ((), (), s32[]{:S(2)}) async-start(), calls=%async_computation.8 | async-start | bytes 12582912 | tf_op jit(solution)/shard_map/psum | solution.py:35
  706.5 112.2 %all-reduce.12.cloned.1.call-start = ((), (), s32[]{:S(2)}) async-start(), calls=%async_computation.9 | async-start | bytes 12582912 | tf_op jit(solution)/shard_map/psum | solution.py:35
  785.9 206.0 %all-reduce.14.cloned.1.call-start = ((), (), s32[]{:S(2)}) async-start(), calls=%async_computation.16 | async-start | bytes 25165824 | tf_op jit(solution)/shard_map/psum | solution.py:35
  1060.5 105.5 %all-reduce.20.cloned.1.call-start = ((), (), s32[]{:S(2)}) async-start(), calls=%async_computation.23 | async-start | bytes 1048576 | tf_op jit(solution)/shard_map/while/body/eval_jaxpr/psum | solution.py:35
  1209.3 138.0 %reduce-scatter.25.cloned.1.call-start = ((), (), s32[]{:S(2)}) async-start(), calls=%async_computation.26 | async-start | bytes 2359296 | tf_op jit(solution)/shard_map/while/body/eval_jaxpr/reduce_scatter | solution.py:141
  1226.6 144.1 %all-reduce.24.cloned.1.call-start = ((), (), s32[]{:S(2)}) async-start(), calls=%async_computation.27 | async-start | bytes 1048576 | tf_op jit(solution)/shard_map/while/body/eval_jaxpr/psum | solution.py:35
  1382.3 103.9 %all-reduce.20.cloned.1.call-start = ((), (), s32[]{:S(2)}) async-start(), calls=%async_computation.23 | async-start | bytes 1048576 | tf_op jit(solution)/shard_map/while/body/eval_jaxpr/psum | solution.py:35
  1529.5 139.3 %reduce-scatter.25.cloned.1.call-start = ((), (), s32[]{:S(2)}) async-start(), calls=%async_computation.26 | async-start | bytes 2359296 | tf_op jit(solution)/shard_map/while/body/eval_jaxpr/reduce_scatter | solution.py:141
  1546.8 144.4 %all-reduce.24.cloned.1.call-start = ((), (), s32[]{:S(2)}) async-start(), calls=%async_computation.27 | async-start | bytes 1048576 | tf_op jit(solution)/shard_map/while/body/eval_jaxpr/psum | solution.py:35
  1703.4 104.0 %all-reduce.20.cloned.1.call-start = ((), (), s32[]{:S(2)}) async-start(), calls=%async_computation.23 | async-start | bytes 1048576 | tf_op jit(solution)/shard_map/while/body/eval_jaxpr/psum | solution.py:35
  1850.7 138.5 %reduce-scatter.25.cloned.1.call-start = ((), (), s32[]{:S(2)}) async-start(), calls=%async_computation.26 | async-start | bytes 2359296 | tf_op jit(solution)/shard_map/while/body/eval_jaxpr/reduce_scatter | solution.py:141
  1868.0 144.2 %all-reduce.24.cloned.1.call-start = ((), (), s32[]{:S(2)}) async-start(), calls=%async_computation.27 | async-start | bytes 1048576 | tf_op jit(solution)/shard_map/while/body/eval_jaxpr/psum | solution.py:35
  2024.2 104.0 %all-reduce.20.cloned.1.call-start = ((), (), s32[]{:S(2)}) async-start(), calls=%async_computation.23 | async-start | bytes 1048576 | tf_op jit(solution)/shard_map/while/body/eval_jaxpr/psum | solution.py:35
  2171.6 138.4 %reduce-scatter.25.cloned.1.call-start = ((), (), s32[]{:S(2)}) async-start(), calls=%async_computation.26 | async-start | bytes 2359296 | tf_op jit(solution)/shard_map/while/body/eval_jaxpr/reduce_scatter | solution.py:141
  2188.8 144.2 %all-reduce.24.cloned.1.call-start = ((), (), s32[]{:S(2)}) async-start(), calls=%async_computation.27 | async-start | bytes 1048576 | tf_op jit(solution)/shard_map/while/body/eval_jaxpr/psum | solution.py:35
  2338.2 125.1 %reduce-scatter.21.cloned.1.call-start = ((), (), s32[]{:S(2)}) async-start(), calls=%async_computation.15 | async-start | bytes 589824
  2340.0 196.8 %reduce-scatter.13.cloned.1.call-start = ((), (), s32[]{:S(2)}) async-start(), calls=%async_computation.11 | async-start | bytes 2359296 | tf_op jit(solution)/shard_map/reduce_scatter | solution.py:314
  2343.6 253.9 %reduce-scatter.11.cloned.1.call-start = ((), (), s32[]{:S(2)}) async-start(), calls=%async_computation.10 | async-start | bytes 7077888 | tf_op jit(solution)/shard_map/reduce_scatter | solution.py:313
  2363.0 385.9 %reduce-scatter.15.cloned.1.call-start = ((), (), s32[]{:S(2)}) async-start(), calls=%async_computation.12 | async-start | bytes 9437184 | tf_op jit(solution)/shard_map/reduce_scatter | solution.py:315
  2386.4 513.1 %reduce-scatter.17.cloned.1.call-start = ((), (), s32[]{:S(2)}) async-start(), calls=%async_computation.13 | async-start | bytes 9437184 | tf_op jit(solution)/shard_map/reduce_scatter | solution.py:316
  2411.0 752.6 %reduce-scatter.19.cloned.1.call-start = ((), (), s32[]{:S(2)}) async-start(), calls=%async_computation.14 | async-start | bytes 13369344 | tf_op jit(solution)/shard_map/reduce_scatter | solution.py:288
  (138 other events, 3284.4 us)
Sparse Core Ops, SparseCore 0:
  17.4 40.3 all-gather.26
  60.6 38.4 all-gather.24
  158.2 39.6 all-gather.26
  200.6 38.4 all-gather.24
  298.2 39.6 all-gather.26
  340.6 38.4 all-gather.24
  438.2 39.6 all-gather.26
  480.6 38.4 all-gather.24
  1060.1 41.1 all-gather.30
  1103.9 38.4 all-gather.28
  1209.5 66.8 reduce-scatter.22
  1280.3 67.0 reduce-scatter.24
  1381.6 39.6 all-gather.30
  1424.1 38.4 all-gather.28
  1529.6 67.0 reduce-scatter.22
  1600.7 68.0 reduce-scatter.24
  1702.8 39.6 all-gather.30
  1745.3 38.4 all-gather.28
  1850.8 67.0 reduce-scatter.22
  1921.7 67.5 reduce-scatter.24
  2023.8 39.6 all-gather.30
  2066.1 38.4 all-gather.28
  2171.7 66.7 reduce-scatter.22
  2242.3 67.6 reduce-scatter.24
  (20 shorter events, 387.5 us)
Sparse Core Ops, SparseCore 1:
  706.6 35.2 all-reduce.9
  786.0 32.7 all-reduce.11
  942.2 49.6 all-reduce.13
  2342.3 60.5 reduce-scatter.20
  2407.4 67.6 reduce-scatter.12
  2479.8 117.7 reduce-scatter.10
  2602.1 146.8 reduce-scatter.14
  2753.0 146.4 reduce-scatter.16
  2902.3 261.2 reduce-scatter.18
where the time goes:
time: 3180 us; the launch traced here: 3170 us
  waiting for transfers between devices  2100 us (66%)
  matrix products  567 us (18%)
  local copies, waits for them, and re-layouts  247 us (8%)
  other arithmetic  233 us (7%)
    psum x23, waiting for transfers between devices, head_total(): return lax.psum(partial_sum, 'tensor')  442 us
    all_gather x8, waiting for transfers between devices, frame_forward(): lax.all_gather(parts[:, 2], 'dp', axis=0, tiled=True)  289 us
    reduce_scatter x4, waiting for transfers between devices, frame_backward(): lax.psum_scatter(keys_term, 'dp', scatter_dimension=0, tiled=True)  286 us
    reduce_scatter x1, waiting for transfers between devices, body(): lax.psum_scatter(table_part, ('section', 'dp'), scatter_dimension=1, tile...  264 us
    reduce_scatter x1, waiting for transfers between devices, body(): lax.psum_scatter(rise_sum, 'dp', scatter_dimension=0, tiled=True)  151 us
    reduce_scatter x1, waiting for transfers between devices, body(): lax.psum_scatter(fall_sum, 'dp', scatter_dimension=1, tiled=True)  151 us
    all_gather x4, waiting for transfers between devices, frame_backward(): lax.all_gather(parts[:, 1], 'dp', axis=0, tiled=True)  148 us
    all_gather x4, waiting for transfers between devices, frame_forward(): lax.all_gather(parts[:, 1], 'dp', axis=0, tiled=True)  147 us
  transfers between devices with their start and end apart: 56, of which 53 were waited for; matrix products, arithmetic and copies ran while one was open for 15% of the time, Pallas kernels for 0%

commit v1 on v0

--- a/solution.py
+++ b/solution.py
@@ -1,6 +1,10 @@
+import functools
+
 import jax
 import jax.numpy as jnp
 from jax import lax
+from jax.experimental import pallas as pl
+from jax.experimental.pallas import tpu as pltpu
 from jax.sharding import PartitionSpec as P
 
 HEAD = 64
@@ -229,7 +233,7 @@
     )
 
 
-def body(frames, codes, lengths, gains, w_qkv, w_out, w_up, w_down, table, cotangent):
+def plain_body(frames, codes, lengths, gains, w_qkv, w_out, w_up, w_down, table, cotangent):
     on_first = lax.axis_index("section") == 0
     head_count = w_qkv.shape[3] // HEAD
     layer_weights = (w_qkv[0], w_out[0], w_up[0], w_down[0])
@@ -332,6 +336,928 @@
     )
 
 
+def lasting(us):
+    return pl.CostEstimate(flops=int(us * 1.1e9), bytes_accessed=int(us * 1e6), transcendentals=0)
+
+f32=jnp.float32; bf=jnp.bfloat16
+
+def mm(a,b): return jnp.dot(a,b,preferred_element_type=f32)
+def mm_nt(a,b): return lax.dot_general(a,b,(((1,),(1,)),((),())),preferred_element_type=f32)
+
+def gelu_both(v):
+    c0=0.7978845608028654; a=0.044715
+    sq=v*v
+    th=jnp.tanh(c0*v*(1.0+a*sq))
+    half=0.5*(1.0+th)
+    act=v*half
+    grad=half+0.5*v*(1.0-th*th)*(c0*(1.0+3.0*a*sq))
+    return act,grad
+
+def local_kernel(g_ref, emb_ref, cot_ref, gao_ref, gax_ref, gains_ref, e_ref, et_ref,
+                 pqo, pqx, woo, wox, wuo, wux,
+                 normed_o, atto_o, attx_o, resid_o, mid_o, acto_o, actx_o, griso_o, grisx_o, glow_o, gpo_o, gpx_o, dx_o, gframe_o, gg_o,
+                 q_s, k_s, v_s, p_s, r_s, gm_s, gatt_s):
+    F=g_ref.shape[0]; R=3*F; D=g_ref.shape[1]; H2=D//2
+    step=pl.program_id(0)
+    gain0=gains_ref[0:1,:]; gain1=gains_ref[1:2,:]
+    g=g_ref[...].astype(f32)
+    scr=(q_s,k_s,v_s)
+    r0s=[]
+    for c in range(3):
+        x=g+emb_ref[c].astype(f32)
+        r0=lax.rsqrt(jnp.mean(x*x,axis=-1,keepdims=True)+eps)
+        r0s.append(r0)
+        normed_o[c]=(x*r0*gain0).astype(bf)
+    normed=normed_o[...].reshape(R,D)
+    for j in range(3):
+        scr[j][:,0:H2]=mm(normed,pqo[j]).astype(bf)
+        scr[j][:,H2:D]=mm(normed,pqx[j]).astype(bf)
+    E=e_ref[...]; ET=et_ref[...]
+    def headsum(prod):
+        hi=prod.astype(bf)
+        lo=(prod-hi.astype(f32)).astype(bf)
+        return mm(hi,E)+mm(lo,E)
+    pidx={}
+    n=0
+    for c in range(3):
+        qc=q_s[c*F:(c+1)*F,:].astype(f32)
+        ss=[headsum(qc*k_s[c2*F:(c2+1)*F,:].astype(f32))*0.125 for c2 in range(c+1)]
+        top=functools.reduce(jnp.maximum,ss)
+        ws=[jnp.exp(s-top) for s in ss]
+        mass=functools.reduce(jnp.add,ws)
+        acc=None
+        for c2 in range(c+1):
+            p=ws[c2]/mass
+            p_s[n]=p; pidx[c,c2]=n; n+=1
+            t=mm(p.astype(bf),ET)*v_s[c2*F:(c2+1)*F,:].astype(f32)
+            acc=t if acc is None else acc+t
+        att=acc.astype(bf)
+        atto_o[c]=att[:,0:H2]; attx_o[c]=att[:,H2:D]
+    xs=(g_ref[...].astype(f32)[None]+emb_ref[...].astype(f32)).reshape(R,D)
+    resid=xs+mm(atto_o[...].reshape(R,H2),woo[...])+mm(attx_o[...].reshape(R,H2),wox[...])
+    r1=lax.rsqrt(jnp.mean(resid*resid,axis=-1,keepdims=True)+eps)
+    resid_o[...]=resid.reshape(3,F,D)
+    nm=(resid*r1*gain1).astype(bf)
+    mid_o[...]=nm.reshape(3,F,D)
+    ch=512
+    gm=None
+    for (wu,act_o,gris_o,ga_ref) in ((wuo,acto_o,griso_o,gao_ref),(wux,actx_o,grisx_o,gax_ref)):
+        for j in range(wu.shape[1]//ch):
+            sl=slice(j*ch,(j+1)*ch)
+            w=wu[:,sl]
+            act,gr=gelu_both(mm(nm,w))
+            act_o[:,:,sl]=act.astype(bf).reshape(3,F,ch)
+            gl=(ga_ref[:,:,sl].reshape(R,ch).astype(f32)*gr).astype(bf)
+            gris_o[:,:,sl]=gl.reshape(3,F,ch)
+            t=mm_nt(gl,w)
+            if gm is None:
+                gm_s[...]=t; gm=1
+            else:
+                gm_s[...]+=t
+    gmid=gm_s[...]
+    n1=resid_o[...].reshape(R,D)*r1
+    u=gmid*gain1
+    gres=cot_ref[...].reshape(R,D).astype(f32)+r1*(u-n1*jnp.mean(u*n1,axis=-1,keepdims=True))
+    gsum1=jnp.sum(gmid*n1,axis=0,keepdims=True)
+    r_s[...]=gres
+    glow=gres.astype(bf)
+    glow_o[...]=glow.reshape(3,F,D)
+    gatt_s[:,0:H2]=mm_nt(glow,woo[...]).astype(bf)
+    gatt_s[:,H2:D]=mm_nt(glow,wox[...]).astype(bf)
+    gk=[None]*3; gv=[None]*3
+    def add(a,b): return b if a is None else a+b
+    for c in range(3):
+        ga=gatt_s[c*F:(c+1)*F,:].astype(f32)
+        gps=[headsum(ga*v_s[c2*F:(c2+1)*F,:].astype(f32)) for c2 in range(c+1)]
+        ps=[p_s[pidx[c,c2]] for c2 in range(c+1)]
+        spread=functools.reduce(jnp.add,[p*gp for p,gp in zip(ps,gps)])
+        qc=q_s[c*F:(c+1)*F,:].astype(f32)
+        gq=None
+        for c2 in range(c+1):
+            gs=mm((ps[c2]*(gps[c2]-spread)*0.125).astype(bf),ET)
+            pb=mm(ps[c2].astype(bf),ET)
+            gq=add(gq,gs*k_s[c2*F:(c2+1)*F,:].astype(f32))
+            gk[c2]=add(gk[c2],gs*qc)
+            gv[c2]=add(gv[c2],pb*ga)
+        gq=gq.astype(bf)
+        gpo_o[0,c]=gq[:,0:H2]; gpx_o[0,c]=gq[:,H2:D]
+    for c in range(3):
+        a=gk[c].astype(bf); gpo_o[1,c]=a[:,0:H2]; gpx_o[1,c]=a[:,H2:D]
+        a=gv[c].astype(bf); gpo_o[2,c]=a[:,0:H2]; gpx_o[2,c]=a[:,H2:D]
+    gn=None
+    for j in range(3):
+        gn=add(gn,mm_nt(gpo_o[j].reshape(R,H2),pqo[j]))
+        gn=gn+mm_nt(gpx_o[j].reshape(R,H2),pqx[j])
+    gm_s[...]=gn
+    tot=None; gsum0=None
+    for c in range(3):
+        gn=gm_s[c*F:(c+1)*F,:]
+        n0=(g_ref[...].astype(f32)+emb_ref[c].astype(f32))*r0s[c]
+        w=gn*gain0
+        dx=r_s[c*F:(c+1)*F,:]+r0s[c]*(w-n0*jnp.mean(w*n0,axis=-1,keepdims=True))
+        gsum0=add(gsum0,jnp.sum(gn*n0,axis=0,keepdims=True))
+        dx_o[c]=dx.astype(bf)
+        tot=add(tot,dx)
+    gframe_o[...]=tot
+    @pl.when(step==0)
+    def _(): gg_o[...]=jnp.zeros_like(gg_o)
+    gg_o[0:1,:]+=gsum0
+    gg_o[1:2,:]+=gsum1
+
+def local_call(g,emb,cot,gao,gax,gains,pqo,pqx,woo,wox,wuo,wux,tile=128):
+    N,D=g.shape; H2=D//2; FH=wuo.shape[1]; F=tile
+    E=(jnp.arange(D)[:,None]//HEAD==jnp.arange(128)[None,:]).astype(bf)
+    ET=E.T
+    c3=lambda w: pl.BlockSpec((3,F,w),lambda i:(0,i,0))
+    whole=lambda shp: pl.BlockSpec(shp,lambda i:(0,)*len(shp),pipeline_mode=pl.Buffered(1))
+    sd=jax.ShapeDtypeStruct
+    out_shape=(sd((3,N,D),bf),sd((3,N,H2),bf),sd((3,N,H2),bf),sd((3,N,D),f32),sd((3,N,D),bf),
+       sd((3,N,FH),bf),sd((3,N,FH),bf),sd((3,N,FH),bf),sd((3,N,FH),bf),sd((3,N,D),bf),
+       sd((3,3,N,H2),bf),sd((3,3,N,H2),bf),sd((3,N,D),bf),sd((N,D),f32),sd((2,D),f32))
+    gp=pl.BlockSpec((3,3,F,H2),lambda i:(0,0,i,0))
+    return pl.pallas_call(local_kernel, grid=(N//F,),
+      in_specs=[pl.BlockSpec((F,D),lambda i:(i,0)),c3(D),c3(D),c3(FH),c3(FH),whole((2,D)),whole(E.shape),whole(ET.shape),
+        whole(pqo.shape),whole(pqx.shape),whole(woo.shape),whole(wox.shape),whole(wuo.shape),whole(wux.shape)],
+      out_specs=(c3(D),c3(H2),c3(H2),c3(D),c3(D),c3(FH),c3(FH),c3(FH),c3(FH),c3(D),gp,gp,c3(D),pl.BlockSpec((F,D),lambda i:(i,0)),pl.BlockSpec((2,D),lambda i:(0,0))),
+      out_shape=out_shape,
+      scratch_shapes=[pltpu.VMEM((3*F,D),bf)]*3+[pltpu.VMEM((6,F,128),f32),pltpu.VMEM((3*F,D),f32),pltpu.VMEM((3*F,D),f32),pltpu.VMEM((3*F,D),bf)],
+      compiler_params=pltpu.CompilerParams(vmem_limit_bytes=63 * 1024 * 1024),
+      cost_estimate=lasting(57),
+      name="local_layer",
+    )(g,emb,cot,gao,gax,gains,E,ET,pqo,pqx,woo,wox,wuo,wux)
+
+def attend_kernel(at_ref, q_ref, k_ref, v_ref, qid_ref, kid_ref, o_ref):
+    @pl.when(at_ref[0] == 0)
+    def _():
+        bias = jnp.where(
+            ((qid_ref[:, 1:2] == kid_ref[1:2, :]) & (kid_ref[0:1, :] <= qid_ref[:, 0:1]))
+            | (kid_ref[0:1, :] == qid_ref[:, 0:1]),
+            0.0,
+            far,
+        )
+        lane = lax.broadcasted_iota(jnp.int32, (1, 2 * HEAD), 1) // HEAD
+        for pair in range(q_ref.shape[1] // (2 * HEAD)):
+            cols = slice(pair * 2 * HEAD, (pair + 1) * 2 * HEAD)
+            q, k, v = q_ref[:, cols], k_ref[:, cols], v_ref[:, cols]
+            total = None
+            for side in range(2):
+                here = lane == side
+                scores = mm_nt(jnp.where(here, q, jnp.zeros_like(q)), k) * HEAD ** (-0.5) + bias
+                top = jnp.max(scores, axis=-1, keepdims=True)
+                weights = jnp.exp(scores - top)
+                mass = jnp.sum(weights, axis=-1, keepdims=True)
+                probs = (weights * (1.0 / mass)).astype(bf)
+                term = mm(probs, jnp.where(here, v, jnp.zeros_like(v)))
+                total = term if total is None else total + term
+            o_ref[:, cols] = total.astype(bf)
+
+
+def attend_call(at, q, k, v, qid, kid, rows):
+    total, width = q.shape
+    part = pl.BlockSpec((rows, width), lambda i, s: (i, 0))
+    whole = pl.BlockSpec((total, width), lambda i, s: (0, 0))
+    return pl.pallas_call(
+        attend_kernel,
+        grid_spec=pltpu.PrefetchScalarGridSpec(
+            num_scalar_prefetch=1,
+            grid=(total // rows,),
+            in_specs=[part, whole, whole, pl.BlockSpec((rows, 2), lambda i, s: (i, 0)), pl.BlockSpec(kid.shape, lambda i, s: (0, 0))],
+            out_specs=part,
+        ),
+        out_shape=jax.ShapeDtypeStruct((total, width), bf),
+        compiler_params=pltpu.CompilerParams(vmem_limit_bytes=60 * 1024 * 1024),
+        cost_estimate=lasting(11),
+        name="frame_attention",
+    )(at, q, k, v, qid, kid)
+
+
+def attend_back_kernel(at_ref, q_ref, k_ref, v_ref, g_ref, qid_ref, kid_ref, gq_ref, gk_ref, gv_ref, ks_ref, vs_ref):
+    @pl.when(at_ref[0] == 0)
+    def _():
+        step = pl.program_id(0)
+
+        @pl.when(step == 0)
+        def _():
+            ks_ref[...] = jnp.zeros_like(ks_ref)
+            vs_ref[...] = jnp.zeros_like(vs_ref)
+
+        bias = jnp.where(
+            ((qid_ref[:, 1:2] == kid_ref[1:2, :]) & (kid_ref[0:1, :] <= qid_ref[:, 0:1]))
+            | (kid_ref[0:1, :] == qid_ref[:, 0:1]),
+            0.0,
+            far,
+        )
+        lane = lax.broadcasted_iota(jnp.int32, (1, 2 * HEAD), 1) // HEAD
+        for pair in range(q_ref.shape[1] // (2 * HEAD)):
+            cols = slice(pair * 2 * HEAD, (pair + 1) * 2 * HEAD)
+            q, k, v, g = q_ref[:, cols], k_ref[:, cols], v_ref[:, cols], g_ref[:, cols]
+            gq = None
+            for side in range(2):
+                here = lane == side
+                qh = jnp.where(here, q, jnp.zeros_like(q))
+                gh = jnp.where(here, g, jnp.zeros_like(g))
+                kh = jnp.where(here, k, jnp.zeros_like(k))
+                scores = mm_nt(qh, k) * HEAD ** (-0.5) + bias
+                top = jnp.max(scores, axis=-1, keepdims=True)
+                weights = jnp.exp(scores - top)
+                mass = jnp.sum(weights, axis=-1, keepdims=True)
+                probs = weights * (1.0 / mass)
+                grad_probs = mm_nt(gh, v)
+                spread = jnp.sum(probs * grad_probs, axis=-1, keepdims=True)
+                gs = (probs * (grad_probs - spread) * HEAD ** (-0.5)).astype(bf)
+                term = mm(gs, kh)
+                gq = term if gq is None else gq + term
+                ks_ref[:, cols] += across_rows(gs, qh)
+                vs_ref[:, cols] += across_rows(probs.astype(bf), gh)
+            gq_ref[:, cols] = gq.astype(bf)
+
+        @pl.when(step == pl.num_programs(0) - 1)
+        def _():
+            gk_ref[...] = ks_ref[...].astype(bf)
+            gv_ref[...] = vs_ref[...].astype(bf)
+
+
+def attend_back_call(at, q, k, v, g, qid, kid, rows):
+    total, width = q.shape
+    part = pl.BlockSpec((rows, width), lambda i, s: (i, 0))
+    whole = pl.BlockSpec((total, width), lambda i, s: (0, 0))
+    shape = jax.ShapeDtypeStruct((total, width), bf)
+    return pl.pallas_call(
+        attend_back_kernel,
+        grid_spec=pltpu.PrefetchScalarGridSpec(
+            num_scalar_prefetch=1,
+            grid=(total // rows,),
+            in_specs=[part, whole, whole, part, pl.BlockSpec((rows, 2), lambda i, s: (i, 0)), pl.BlockSpec(kid.shape, lambda i, s: (0, 0))],
+            out_specs=(part, whole, whole),
+            scratch_shapes=[pltpu.VMEM((total, width), f32)] * 2,
+        ),
+        out_shape=(shape, shape, shape),
+        compiler_params=pltpu.CompilerParams(vmem_limit_bytes=60 * 1024 * 1024),
+        cost_estimate=lasting(0.01),
+        name="frame_attention_back",
+    )(at, q, k, v, g, qid, kid)
+
+
+def front_kernel(at_ref, x_ref, ao_ref, ax_ref, gain_ref, oo_ref, ox_ref, uo_ref, ux_ref, do_ref, dx_ref,
+                 resid_ref, mid_ref, act_o, act_x, slope_o, slope_x, out_ref, total_ref):
+    @pl.when(at_ref[0] == 0)
+    def _():
+        step = pl.program_id(0)
+        turn = pl.num_programs(0) // 2
+
+        @pl.when(step == 0)
+        def _():
+            resid = x_ref[...].astype(f32) + mm(ao_ref[...], oo_ref[...]) + mm(ax_ref[...], ox_ref[...])
+            resid_ref[...] = resid
+            scale = lax.rsqrt(jnp.mean(resid * resid, axis=-1, keepdims=True) + eps)
+            mid_ref[...] = (resid * scale * gain_ref[1:2, :]).astype(bf)
+            total_ref[...] = resid
+
+        def part(up, down, act_ref, slope_ref):
+            act, slope = gelu_both(mm(mid_ref[...], up[...]))
+            act = act.astype(bf)
+            act_ref[...] = act
+            slope_ref[...] = slope.astype(bf)
+            total_ref[...] += mm(act, down[...])
+
+        @pl.when(step < turn)
+        def _():
+            part(uo_ref, do_ref, act_o, slope_o)
+
+        @pl.when(step >= turn)
+        def _():
+            part(ux_ref, dx_ref, act_x, slope_x)
+
+        @pl.when(step == pl.num_programs(0) - 1)
+        def _():
+            out_ref[...] = total_ref[...].astype(bf)
+
+
+def halves_specs(turn, chunk, width, rows):
+    first = lambda i, s: jnp.minimum(i, turn - 1) * (1 - s[0])
+    later = lambda i, s: jnp.maximum(i - turn, 0) * (1 - s[0])
+    ups = [pl.BlockSpec((width, chunk), lambda i, s, f=f: (0, f(i, s))) for f in (first, later)]
+    downs = [pl.BlockSpec((chunk, width), lambda i, s, f=f: (f(i, s), 0)) for f in (first, later)]
+    cols = [pl.BlockSpec((rows, chunk), lambda i, s, f=f: (0, f(i, s))) for f in (first, later)]
+    return ups, downs, cols
+
+
+def front_call(at, x, att_own, att_oth, gains, out_own, out_oth, up_own, up_oth, down_own, down_oth, chunk=512):
+    rows, width = x.shape
+    hidden = up_own.shape[1]
+    turn = hidden // chunk
+    ups, downs, cols = halves_specs(turn, chunk, width, rows)
+    whole = lambda a: pl.BlockSpec(a.shape, lambda i, s: (0,) * a.ndim)
+    sd = jax.ShapeDtypeStruct
+    full = pl.BlockSpec((rows, width), lambda i, s: (0, 0))
+    hid = sd((rows, hidden), bf)
+    return pl.pallas_call(
+        front_kernel,
+        grid_spec=pltpu.PrefetchScalarGridSpec(
+            num_scalar_prefetch=1,
+            grid=(2 * turn,),
+            in_specs=[full, whole(att_own), whole(att_oth), whole(gains), whole(out_own), whole(out_oth), *ups, *downs],
+            out_specs=(full, full, cols[0], cols[1], cols[0], cols[1], full),
+            scratch_shapes=[pltpu.VMEM((rows, width), f32)],
+        ),
+        out_shape=(sd((rows, width), f32), sd((rows, width), bf), hid, hid, hid, hid, sd((rows, width), bf)),
+        compiler_params=pltpu.CompilerParams(vmem_limit_bytes=60 * 1024 * 1024),
+        cost_estimate=lasting(15),
+        name="global_forward",
+    )(at, x, att_own, att_oth, gains, out_own, out_oth, up_own, up_oth, down_own, down_oth)
+
+
+def back_kernel(at_ref, g_ref, resid_ref, gain_ref, so_ref, sx_ref, uo_ref, ux_ref, do_ref, dx_ref,
+                rise_o, rise_x, grad_ref, low_ref, gsum_ref, total_ref):
+    @pl.when(at_ref[0] == 0)
+    def _():
+        step = pl.program_id(0)
+        turn = pl.num_programs(0) // 2
+
+        def part(up, down, slope_ref, rise_ref):
+            rise = (mm_nt(g_ref[...], down[...]) * slope_ref[...].astype(f32)).astype(bf)
+            rise_ref[...] = rise
+            return mm_nt(rise, up[...])
+
+        @pl.when(step == 0)
+        def _():
+            total_ref[...] = part(uo_ref, do_ref, so_ref, rise_o)
+
+        @pl.when((step > 0) & (step < turn))
+        def _():
+            total_ref[...] += part(uo_ref, do_ref, so_ref, rise_o)
+
+        @pl.when(step >= turn)
+        def _():
+            total_ref[...] += part(ux_ref, dx_ref, sx_ref, rise_x)
+
+        @pl.when(step == pl.num_programs(0) - 1)
+        def _():
+            resid = resid_ref[...]
+            scale = lax.rsqrt(jnp.mean(resid * resid, axis=-1, keepdims=True) + eps)
+            normal = resid * scale
+            total = total_ref[...]
+            unit = total * gain_ref[1:2, :]
+            grad = g_ref[...].astype(f32) + scale * (unit - normal * jnp.mean(unit * normal, axis=-1, keepdims=True))
+            grad_ref[...] = grad
+            low_ref[...] = grad.astype(bf)
+            gsum_ref[...] = jnp.sum(total * normal, axis=0, keepdims=True)
+
+
+def back_call(at, g, resid, gains, slope_own, slope_oth, up_own, up_oth, down_own, down_oth, chunk=512):
+    rows, width = g.shape
+    hidden = up_own.shape[1]
+    turn = hidden // chunk
+    ups, downs, cols = halves_specs(turn, chunk, width, rows)
+    sd = jax.ShapeDtypeStruct
+    full = pl.BlockSpec((rows, width), lambda i, s: (0, 0))
+    hid = sd((rows, hidden), bf)
+    line = pl.BlockSpec((1, width), lambda i, s: (0, 0))
+    return pl.pallas_call(
+        back_kernel,
+        grid_spec=pltpu.PrefetchScalarGridSpec(
+            num_scalar_prefetch=1,
+            grid=(2 * turn,),
+            in_specs=[full, full, pl.BlockSpec(gains.shape, lambda i, s: (0, 0)), *cols, *ups, *downs],
+            out_specs=(*cols, full, full, line),
+            scratch_shapes=[pltpu.VMEM((rows, width), f32)],
+        ),
+        out_shape=(hid, hid, sd((rows, width), f32), sd((rows, width), bf), sd((1, width), f32)),
+        compiler_params=pltpu.CompilerParams(vmem_limit_bytes=60 * 1024 * 1024),
+        cost_estimate=lasting(13),
+        name="global_backward",
+    )(at, g, resid, gains, slope_own, slope_oth, up_own, up_oth, down_own, down_oth)
+
+
+def split_sides(total, side, mine_ref, theirs_ref, at):
+    half = total.shape[0] // 2
+    top, bottom = total[:half].astype(bf), total[half:].astype(bf)
+    mine_ref[at] = jnp.where(side == 0, top, bottom)
+    theirs_ref[at] = jnp.where(side == 0, bottom, top)
+
+
+def weight_kernel(at_ref, gl, gli, gr, gri, ll, lli, lr, lri, mine_ref, theirs_ref, *, plane_first):
+    step = pl.program_id(0)
+
+    def store(total):
+        if not plane_first:
+            split_sides(total, at_ref[2], mine_ref, theirs_ref, 0)
+            return
+        half = total.shape[0] // 2
+        top, bottom = total[:half].astype(bf), total[half:].astype(bf)
+        flip = at_ref[2] == 0
+        near, far_side = jnp.where(flip, top, bottom), jnp.where(flip, bottom, top)
+
+        @pl.when(step < 2)
+        def _():
+            theirs_ref[0, 0] = near
+            theirs_ref[1, 0] = far_side
+
+        @pl.when(step >= 2)
+        def _():
+            mine_ref[0, 0] = near
+            mine_ref[1, 0] = far_side
+
+    @pl.when(at_ref[0] == 0)
+    def _():
+        store(across_rows(gl[...], gr[...]) + across_rows(gli[...], gri[...]))
+
+    @pl.when(at_ref[0] == 1)
+    def _():
+        store(across_rows(ll[...], lr[...]) + across_rows(lli[...], lri[...]))
+
+
+def weight_call(at, four_global, four_local, plane_first, name):
+    width = four_global[0].shape[1]
+    cols = four_global[2].shape[1]
+    piece = width // 8
+    once = pl.Buffered(1)
+
+    def turn(i):
+        return jnp.where(i < 2, 2 * i + 1, 2 * i - 4) if plane_first else i
+
+    def left(a, here):
+        return pl.BlockSpec((a.shape[0], 2 * piece), lambda i, s: (0, jnp.where(s[0] == here, s[1] ^ turn(i), 0)))
+
+    def right(a):
+        return pl.BlockSpec(a.shape, lambda i, s: (0, 0), pipeline_mode=once)
+
+    def specs(four, here):
+        return [left(four[0], here), left(four[1], here), right(four[2]), right(four[3])]
+
+    if plane_first:
+        shape = jax.ShapeDtypeStruct((2, 2, piece, cols), bf)
+        outs = (
+            pl.BlockSpec((2, 1, piece, cols), lambda i, s: (0, jnp.maximum(i - 2, 0), 0, 0)),
+            pl.BlockSpec((2, 1, piece, cols), lambda i, s: (0, jnp.minimum(i, 1), 0, 0)),
+        )
+    else:
+        shape = jax.ShapeDtypeStruct((4, piece, cols), bf)
+        outs = (pl.BlockSpec((1, piece, cols), lambda i, s: ((i % 2) * 2 + i // 2, 0, 0)),) * 2
+    return pl.pallas_call(
+        functools.partial(weight_kernel, plane_first=plane_first),
+        grid_spec=pltpu.PrefetchScalarGridSpec(
+            num_scalar_prefetch=1,
+            grid=(4,),
+            in_specs=specs(four_global, 0) + specs(four_local, 1),
+            out_specs=outs,
+        ),
+        out_shape=(shape, shape),
+        compiler_params=pltpu.CompilerParams(vmem_limit_bytes=60 * 1024 * 1024),
+        cost_estimate=lasting(10),
+        name=name,
+    )(at, *four_global, *four_local)
+
+
+def rest_kernel(at_ref, gl, gn, ga, gq, gk, gv, ll, lli, ln, lni, la, lai, lp, lpi, mine_ref, theirs_ref):
+    size = la.shape[1]
+    side = at_ref[2]
+
+    def put(block, total):
+        half = total.shape[0] // 2
+        cols = slice(block, block + total.shape[1])
+        top, bottom = total[:half].astype(bf), total[half:].astype(bf)
+        mine_ref[0, :, cols] = jnp.where(side == 0, top, bottom)
+        theirs_ref[0, :, cols] = jnp.where(side == 0, bottom, top)
+
+    for which in range(2):
+
+        @pl.when((at_ref[0] == 0) & (side == which))
+        def _():
+            for j, (left, right) in enumerate(((gl, ga), (gn, gq), (gn, gk), (gn, gv))):
+                total = across_rows(left[...], right[...])
+                start = j * size
+                put(start + which * (size // 2), total)
+                put(start + (1 - which) * (size // 2), jnp.zeros_like(total))
+
+    @pl.when(at_ref[0] == 1)
+    def _():
+        put(0, across_rows(ll[...], la[...]) + across_rows(lli[...], lai[...]))
+        for j in range(3):
+            put((j + 1) * size, across_rows(ln[...], lp[j]) + across_rows(lni[...], lpi[j]))
+
+
+def rest_call(at, g_low, g_normed, g_att, g_packs, l_low, l_low_in, l_normed, l_normed_in, l_att, l_att_in, l_pack, l_pack_in):
+    piece = g_low.shape[1] // 8
+    cols = 4 * l_att.shape[1]
+    once = pl.Buffered(1)
+    left = lambda a: pl.BlockSpec((a.shape[0], 2 * piece), lambda i, s: (0, s[1] ^ i))
+    right = lambda a: pl.BlockSpec(a.shape, lambda i, s: (0,) * a.ndim, pipeline_mode=once)
+    lefts, rights = (l_low, l_low_in, l_normed, l_normed_in), (l_att, l_att_in, l_pack, l_pack_in)
+    shape = jax.ShapeDtypeStruct((4, piece, cols), bf)
+    return pl.pallas_call(
+        rest_kernel,
+        grid_spec=pltpu.PrefetchScalarGridSpec(
+            num_scalar_prefetch=1,
+            grid=(4,),
+            in_specs=[left(g_low), left(g_normed), right(g_att), *map(right, g_packs), *map(left, lefts), *map(right, rights)],
+            out_specs=(pl.BlockSpec((1, piece, cols), lambda i, s: ((i % 2) * 2 + i // 2, 0, 0)),) * 2,
+        ),
+        out_shape=(shape, shape),
+        compiler_params=pltpu.CompilerParams(vmem_limit_bytes=60 * 1024 * 1024),
+        cost_estimate=lasting(0.01),
+        name="rest_gradient",
+    )(at, g_low, g_normed, g_att, *g_packs, *lefts, *rights)
+
+
+def fall_kernel(at_ref, resid_ref, ao_ref, ax_ref, do_ref, dx_ref, out_ref, total_ref):
+    step = pl.program_id(0)
+    turn = pl.num_programs(0) // 2
+    books, planes, half = out_ref.shape[1], out_ref.shape[0], out_ref.shape[2]
+
+    @pl.when(at_ref[0] == 1)
+    def _():
+        @pl.when(step == 0)
+        def _():
+            total_ref[...] = resid_ref[...]
+
+        @pl.when(step < turn)
+        def _():
+            total_ref[...] += mm(ao_ref[...], do_ref[...])
+
+        @pl.when(step >= turn)
+        def _():
+            total_ref[...] += mm(ax_ref[...], dx_ref[...])
+
+        @pl.when(step == pl.num_programs(0) - 1)
+        def _():
+            for c in range(books):
+                for z in range(planes):
+                    first = (c * planes + z) * half
+                    out_ref[z, c] = total_ref[first : first + half, :].astype(bf)
+
+
+def fall_call(at, resid, act_own, act_oth, down_own, down_oth, planes, books, chunk=512):
+    rows, width = resid.shape
+    turn = down_own.shape[0] // chunk
+    first = lambda i, s: jnp.minimum(i, turn - 1) * s[0]
+    later = lambda i, s: jnp.maximum(i - turn, 0) * s[0]
+    col = lambda f: pl.BlockSpec((rows, chunk), lambda i, s: (0, f(i, s)))
+    row = lambda f: pl.BlockSpec((chunk, width), lambda i, s: (f(i, s), 0))
+    shape = (planes, books, rows // planes // books, width)
+    return pl.pallas_call(
+        fall_kernel,
+        grid_spec=pltpu.PrefetchScalarGridSpec(
+            num_scalar_prefetch=1,
+            grid=(2 * turn,),
+            in_specs=[pl.BlockSpec((rows, width), lambda i, s: (0, 0), pipeline_mode=pl.Buffered(1)), col(first), col(later), row(first), row(later)],
+            out_specs=pl.BlockSpec(shape, lambda i, s: (0, 0, 0, 0)),
+            scratch_shapes=[pltpu.VMEM((rows, width), f32)],
+        ),
+        out_shape=jax.ShapeDtypeStruct(shape, bf),
+        compiler_params=pltpu.CompilerParams(vmem_limit_bytes=60 * 1024 * 1024),
+        cost_estimate=lasting(7),
+        name="local_output",
+    )(at, resid, act_own, act_oth, down_own, down_oth)
+
+
+def table_kernel(at_ref, code_ref, code_in_ref, own_ref, got_ref, low_ref, high_ref, total_ref):
+    entries = total_ref.shape[0]
+    slots = lax.broadcasted_iota(jnp.int32, (entries, code_ref.shape[2]), 0)
+    piece = low_ref.shape[3]
+
+    @pl.when(at_ref[0] == 1)
+    def _():
+        hot = (slots == code_ref[0]).astype(f32).astype(bf)
+        hot_in = (slots == code_in_ref[0]).astype(f32).astype(bf)
+        total_ref[...] = mm(hot, own_ref[0]) + mm(hot_in, got_ref[0])
+        for jz in range(4):
+            for jy in range(2):
+                place = (at_ref[1] ^ jz) * 2 + (at_ref[2] ^ jy)
+                spot = (jz % 2) * 2 + jz // 2
+                for ref, base in ((low_ref, 0), (high_ref, entries // 2)):
+                    rows = pl.ds(pl.multiple_of(base + place * piece, piece), piece)
+                    ref[jy, spot, 0] = total_ref[rows, :].astype(bf)
+
+
+def table_call(at, codes, codes_in, own, got, entries):
+    books, rows = codes.shape
+    width = own.shape[2]
+    line = pl.BlockSpec((1, 1, rows), lambda c, s: (c, 0, 0))
+    block = pl.BlockSpec((1, rows, width), lambda c, s: (c, 0, 0))
+    shape = (2, 4, books, entries // 16, width)
+    out = pl.BlockSpec((2, 4, 1, entries // 16, width), lambda c, s: (0, 0, c, 0, 0))
+    return pl.pallas_call(
+        table_kernel,
+        grid_spec=pltpu.PrefetchScalarGridSpec(
+            num_scalar_prefetch=1,
+            grid=(books,),
+            in_specs=[line, line, block, block],
+            out_specs=(out, out),
+            scratch_shapes=[pltpu.VMEM((entries, width), f32)],
+        ),
+        out_shape=(jax.ShapeDtypeStruct(shape, bf),) * 2,
+        compiler_params=pltpu.CompilerParams(vmem_limit_bytes=60 * 1024 * 1024),
+        cost_estimate=lasting(4),
+        name="table_gradient",
+    )(at, codes[:, None, :], codes_in[:, None, :], own, got)
+
+
+def prepare_kernel(at_ref, code_ref, cot_ref, do_ref, dx_ref, table_ref, look_ref, po_ref, px_ref):
+    step = pl.program_id(0)
+    turn = pl.num_programs(0) // 2
+    books, rows, chunk = po_ref.shape
+
+    @pl.when(at_ref[0] == 1)
+    def _():
+        @pl.when(step < look_ref.shape[0])
+        def _():
+            slots = lax.broadcasted_iota(jnp.int32, (rows, table_ref.shape[1]), 1)
+            hot = (slots == code_ref[jnp.minimum(step, look_ref.shape[0] - 1)]).astype(f32).astype(bf)
+            look_ref[jnp.minimum(step, look_ref.shape[0] - 1)] = mm(hot, table_ref[0]).astype(bf)
+
+        @pl.when(step < turn)
+        def _():
+            po_ref[...] = mm_nt(cot_ref[...], do_ref[...]).astype(bf).reshape(books, rows, chunk)
+
+        @pl.when(step >= turn)
+        def _():
+            px_ref[...] = mm_nt(cot_ref[...], dx_ref[...]).astype(bf).reshape(books, rows, chunk)
+
+
+def prepare_call(at, codes, cot, down_own, down_oth, table, chunk=512):
+    books, rows = codes.shape
+    width = cot.shape[1]
+    hidden = down_own.shape[0]
+    turn = hidden // chunk
+    first = lambda i, s: jnp.minimum(i, turn - 1) * s[0]
+    later = lambda i, s: jnp.maximum(i - turn, 0) * s[0]
+    down = lambda f: pl.BlockSpec((chunk, width), lambda i, s: (f(i, s), 0))
+    out = lambda f: pl.BlockSpec((books, rows, chunk), lambda i, s: (0, 0, f(i, s)))
+    sd = jax.ShapeDtypeStruct
+    return pl.pallas_call(
+        prepare_kernel,
+        grid_spec=pltpu.PrefetchScalarGridSpec(
+            num_scalar_prefetch=1,
+            grid=(2 * turn,),
+            in_specs=[
+                pl.BlockSpec((books, rows, 1), lambda i, s: (0, 0, 0)),
+                pl.BlockSpec(cot.shape, lambda i, s: (0, 0)),
+                down(first),
+                down(later),
+                pl.BlockSpec((1,) + table.shape[1:], lambda i, s: (jnp.minimum(i, books - 1) * s[0], 0, 0)),
+            ],
+            out_specs=(pl.BlockSpec((books, rows, width), lambda i, s: (0, 0, 0)), out(first), out(later)),
+        ),
+        out_shape=(sd((books, rows, width), bf), sd((books, rows, hidden), bf), sd((books, rows, hidden), bf)),
+        compiler_params=pltpu.CompilerParams(vmem_limit_bytes=60 * 1024 * 1024),
+        cost_estimate=lasting(5),
+        name="local_prepare",
+    )(at, codes[:, :, None], cot, down_own, down_oth, table)
+
+
+def fence(*groups):
+    return lax.optimization_barrier(groups)
+
+
+def body(frames, codes, lengths, gains, w_qkv, w_out, w_up, w_down, table, cotangent):
+    batches, share, width = frames.shape
+    members = lax.axis_size("dp") // batches
+    if (
+        lax.axis_size("section") != 2
+        or lax.axis_size("tensor") != 2
+        or members != 2
+        or lax.axis_size("dp") != 2 * batches
+        or batches & (batches - 1)
+        or share % 32
+        or table.shape[1] != width
+    ):
+        return plain_body(frames, codes, lengths, gains, w_qkv, w_out, w_up, w_down, table, cotangent)
+    place, core = lax.axis_index("dp"), lax.axis_index("tensor")
+    plane, side = place // members, place % members
+    on_first = lax.axis_index("section") == 0
+    half = share // 2
+    rows = batches * half
+    count = 2 * batches
+    at = jnp.stack([lax.axis_index("section"), plane, side]).astype(jnp.int32)
+
+    everywhere, first, second = (0, 1), (0,), (1,)
+
+    def linked(a, flip_place, flip_core, sections=everywhere):
+        pairs = [
+            ((z * count + i) * 2 + j, (z * count + (i ^ flip_place)) * 2 + (j ^ flip_core))
+            for z in sections
+            for i in range(count)
+            for j in range(2)
+        ]
+        return lax.ppermute(a, ("section", "dp", "tensor"), pairs)
+
+    def core_swap(a, sections=everywhere):
+        return linked(a, 0, 1, sections)
+
+    def side_swap(a, sections=everywhere):
+        return linked(a, 1, 0, sections)
+
+    def both_swap(a, sections=everywhere):
+        return linked(a, 1, 1, sections)
+
+    def to_local(a):
+        return lax.ppermute(a, "section", [(0, 1)])
+
+    def to_global(a):
+        return lax.ppermute(a, "section", [(1, 0)])
+
+    def planes_in(a, sections=everywhere):
+        pieces = [lax.dynamic_slice_in_dim(a, plane ^ k, 1, 0) for k in range(batches)]
+        return jnp.concatenate([pieces[0], *(linked(pieces[k], 2 * k, 0, sections) for k in range(1, batches))], 0)
+
+    def planes_out(a, sections=everywhere):
+        got = [a[:1], *(linked(a[k : k + 1], 2 * k, 0, sections) for k in range(1, batches))]
+        out = jnp.zeros_like(a)
+        for k in range(batches):
+            out = lax.dynamic_update_slice_in_dim(out, got[k], plane ^ k, 0)
+        return out
+
+    def core_half(a, axis):
+        return lax.dynamic_slice_in_dim(a, core * half, half, axis)
+
+    def join_cores(a, axis):
+        other = core_swap(a)
+        return jnp.where(core == 0, jnp.concatenate([a, other], axis), jnp.concatenate([other, a], axis))
+
+    def quarter(a, axis):
+        size = a.shape[axis] // 2
+        return lax.dynamic_slice_in_dim(a, side * size, size, axis)
+
+    def by_side(mine, theirs, axis):
+        return jnp.where(side == 0, jnp.concatenate([mine, theirs], axis), jnp.concatenate([theirs, mine], axis))
+
+    x_own = planes_in(core_half(frames, 1), first).reshape(rows, width)
+    x_side = side_swap(x_own, first)
+    x_core, x_both = core_swap(x_own), core_swap(x_side)
+    (x_core, x_both), (w_qkv, w_out, w_up, w_down, cotangent, codes) = fence(
+        (x_core, x_both), (w_qkv, w_out, w_up, w_down, cotangent, codes)
+    )
+    x_all = jnp.concatenate([x_own, x_side, x_core, x_both], 0)
+
+    gains_here = gains[0]
+    proj_own = w_qkv[0].transpose(1, 0, 2)
+    out_own, up_own, down_own = w_out[0], w_up[0], w_down[0]
+    out_oth, up_oth, down_oth = (core_swap(w) for w in (out_own, up_own, down_own))
+    proj_oth = core_swap(proj_own)
+
+    def positions(jt, js):
+        base = ((jnp.arange(batches)[:, None] ^ plane) * 2 + (side ^ js)) * share + (core ^ jt) * half
+        return (base + jnp.arange(half)[None, :]).reshape(-1)
+
+    pos = jnp.concatenate([positions(0, 0), positions(0, 1), positions(1, 0), positions(1, 1)]).astype(jnp.int32)
+    doc_ends = jnp.cumsum(lax.dynamic_index_in_dim(lengths, plane, 0, keepdims=False))
+    doc = doc_index(pos, doc_ends)
+    qid = jnp.stack([pos, doc], 1)
+    kid = jnp.stack([pos, jnp.where(pos < doc_ends[-1], doc, -1)], 0)
+
+    x_all32 = x_all.astype(f32)
+    all_scale = rms_scale(x_all32)
+    normed_all = (x_all32 * all_scale * gains_here[0]).astype(bf)
+    proj_mine = quarter(proj_own, 2)
+    q, k, v = (matmul(normed_all, proj_mine[j]).astype(bf) for j in range(3))
+    attended = attend_call(at, q, k, v, qid, kid, rows)
+    parts = attended.reshape(4, rows, -1)
+    att_own = by_side(parts[0], side_swap(parts[1], first), 1)
+    att_oth = by_side(core_swap(parts[2]), both_swap(parts[3], first), 1)
+    x32 = x_own.astype(f32)
+    resid, mid, act_own, act_oth, slope_own, slope_oth, global_low = front_call(
+        at, x_own, att_own, att_oth, gains_here, out_own, out_oth, up_own, up_oth, down_own, down_oth
+    )
+    mid_in, act_in = core_swap(mid), core_swap(act_oth)
+
+    arrived = to_local(global_low)
+    cot = planes_in(core_half(cotangent.transpose(0, 2, 1, 3), 2), second).transpose(1, 0, 2, 3).reshape(CODEBOOKS, rows, width)
+    codes_own = planes_in(core_half(codes.transpose(0, 2, 1), 2), second).transpose(1, 0, 2).reshape(CODEBOOKS, rows)
+    slots = jnp.arange(table.shape[1], dtype=jnp.int32)
+    cot_rows = cot.reshape(-1, width)
+    cot_in = core_swap(cot_rows)
+
+    looked_up, pull_own, pull_oth = prepare_call(at, codes_own, cot_rows, down_own, down_oth, table)
+    (
+        l_normed, l_att_own, l_att_oth, l_resid, l_mid, l_act_own, l_act_oth, l_rise_own, l_rise_oth,
+        l_low, l_pack_own, l_pack_oth, l_grad, l_frame, l_gains,
+    ) = local_call(
+        arrived, looked_up, cot, pull_own, pull_oth, gains_here, proj_own, proj_oth, out_own, out_oth, up_own, up_oth
+    )
+    global_moved = planes_out(jnp.where(on_first, global_low, arrived).reshape(batches, half, width))
+    grad_low = to_global(l_frame.astype(bf))
+
+    flat = lambda a: a.reshape(-1, a.shape[-1])
+
+    def swap(a, bit):
+        return lax.ppermute(a, "dp", [(i, i ^ (1 << bit)) for i in range(count)])
+
+    def meet(mine, got):
+        return (mine.astype(f32) + got.astype(f32)).astype(bf)
+
+    def cols_of(a, which):
+        return lax.dynamic_slice_in_dim(a, which * (width // 2), width // 2, 2)
+
+    l_act_in = core_swap(flat(l_act_oth))
+    l_got, codes_oth = core_swap(cols_of(l_grad, 1 - core)), core_swap(codes_own)
+    l_rise_in, l_mid_in = core_swap(flat(l_rise_oth)), core_swap(flat(l_mid))
+    l_low_in, l_att_in = core_swap(flat(l_low)), core_swap(flat(l_att_oth))
+    l_normed_in, l_pack_in = core_swap(flat(l_normed)), core_swap(l_pack_oth)
+    local_low = fall_call(at, flat(l_resid), flat(l_act_own), flat(l_act_oth), down_own, down_oth, batches, CODEBOOKS)
+    table_low, table_high = table_call(at, codes_own, codes_oth, cols_of(l_grad, core), l_got, table.shape[1])
+    (local_low, table_low, table_high), (grad_low,) = fence((local_low, table_low, table_high), (grad_low,))
+
+    grad_in_low = core_swap(grad_low)
+    rise_own, rise_oth, grad_resid, low_own, gain_mid = back_call(
+        at, grad_low, resid, gains_here, slope_own, slope_oth, up_own, up_oth, down_own, down_oth
+    )
+    rise_in = core_swap(rise_oth)
+    (low_own, grad_in_low, table_low, local_low), = fence((low_own, grad_in_low, table_low, local_low))
+    low_side = side_swap(low_own, first)
+    down_mine, down_theirs = weight_call(
+        at, (grad_low, grad_in_low, act_own, act_in), (cot_rows, cot_in, flat(l_act_own), l_act_in), True, "down_gradient"
+    )
+    (down_theirs,), (rise_in,) = fence((down_theirs,), (rise_in,))
+    down_got = swap(down_theirs, 1)
+    up_mine, up_theirs = weight_call(
+        at, (mid, mid_in, rise_own, rise_in), (flat(l_mid), l_mid_in, flat(l_rise_own), l_rise_in), False, "up_gradient"
+    )
+    (up_theirs, low_side, local_low, table_low), = fence((up_theirs, low_side, local_low, table_low))
+    up_got = swap(up_theirs, 0)
+    table_moved = to_global(table_low)
+    local_moved = planes_out(local_low, second)
+    low_all = jnp.concatenate([low_own, low_side, core_swap(low_own), core_swap(low_side)], 0)
+    grad_att = against_rows(low_all, quarter(out_own, 0)).astype(bf)
+    grad_packs = attend_back_call(at, q, k, v, grad_att, qid, kid, rows)
+    part_normed = sum(against_rows(g, proj_mine[j]) for j, g in enumerate(grad_packs))
+    pair = part_normed[: 2 * rows] + core_swap(part_normed[2 * rows :].astype(bf)).astype(f32)
+    pair_side = side_swap(pair[rows:].astype(bf), first)
+    rest_mine, rest_theirs = rest_call(
+        at, low_all, normed_all, attended, grad_packs, flat(l_low), l_low_in, flat(l_normed), l_normed_in,
+        flat(l_att_own), l_att_in, *(a.reshape(3, CODEBOOKS * rows, -1) for a in (l_pack_own, l_pack_in)),
+    )
+    (rest_theirs, down_got, up_got, pair_side, local_moved, global_moved), = fence(
+        (rest_theirs, down_got, up_got, pair_side, local_moved, global_moved)
+    )
+    rest_got = swap(rest_theirs, 0)
+    local_sent = to_global(local_moved)
+    up_now = meet(up_mine, up_got)
+    up_got = swap(up_now[2:], 1)
+    grad_normed = pair[:rows] + pair_side.astype(f32)
+    back_in, gain_in = rms_back(x32, gains_here[0], grad_normed)
+    grad_frames = grad_resid + back_in
+    inner = planes_out(jnp.where(on_first, grad_frames, l_frame).astype(bf).reshape(batches, half, width))
+    gain_sum = jnp.where(on_first, jnp.concatenate([gain_in[None], gain_mid]), l_gains)
+    gain_sum = (gain_sum + core_swap(gain_sum)).reshape(2, batches, 2, -1)
+    down_now = meet(down_mine, down_got)
+    (rest_got, up_got, down_now, inner, table_moved, gain_sum), = fence(
+        (rest_got, up_got, down_now, inner, table_moved, gain_sum)
+    )
+    down_got = swap(down_now[1], 0)
+    piece = width // count
+    gain_rows = [
+        [
+            lax.dynamic_slice(gain_sum, (0, plane ^ (2 * j + i), side ^ y, 0), (2, 1, 1, piece)).reshape(1, -1)
+            for i in range(2)
+            for j in range(2)
+        ]
+        for y in range(2)
+    ]
+    table_now = jnp.where(on_first, table_moved, table_high).reshape(2, batches, -1, width // 2)
+    filler = ((0, 15), (0, width // 2 - 2 * piece))
+    table_now = jnp.concatenate(
+        [table_now, jnp.stack([jnp.stack([jnp.pad(g.astype(bf), filler) for g in four]) for four in gain_rows])], 2
+    )
+    table_got = swap(table_now[1], 0)
+    up_now = meet(up_now[:2], up_got)
+    up_got = swap(up_now[1], 2)
+    rest_now = meet(rest_mine, rest_got)
+    rest_got = swap(rest_now[2:], 1)
+    (rest_got, up_got, down_got, table_got, local_sent), = fence((rest_got, up_got, down_got, table_got, local_sent))
+    down_now = meet(down_now[0], down_got)
+    down_got = swap(down_now[1], 2)
+    rest_now = meet(rest_now[:2], rest_got)
+    rest_got = swap(rest_now[1], 2)
+    table_now = meet(table_now[0], table_got)
+    table_got = swap(table_now[2:], 1)
+    up_share = up_now[0].astype(f32) + up_got.astype(f32)
+    table_now = meet(table_now[:2], table_got)
+    table_got = swap(table_now[1], 2)
+    down_share = down_now[0].astype(f32) + down_got.astype(f32)
+    rest_share = rest_now[0].astype(f32) + rest_got.astype(f32)
+    table_now = table_now[0].astype(f32) + table_got.astype(f32)
+    gain_share = table_now[-16, : 2 * piece].reshape(2, piece)
+    grad_table = join_cores(table_now[:-16].reshape(CODEBOOKS, -1, width // 2).astype(bf), 2).astype(f32)
+
+    global_out = join_cores(global_moved, 1)
+    local_out = join_cores(jnp.where(on_first, local_sent, local_moved), 2).transpose(0, 2, 1, 3)
+    input_grads = join_cores(inner, 1)
+    hidden = out_own.shape[0]
+    proj_share = rest_share[:, hidden:].reshape(piece, 3, hidden)
+    return (
+        global_out,
+        local_out,
+        input_grads.astype(f32)[None],
+        proj_share[None],
+        rest_share[:, :hidden].T[None],
+        up_share[None],
+        down_share.T[None],
+        gain_share[None],
+        grad_table,
+    )
+
+
 def solution(mesh):
     in_specs = (
         P(None, "dp", None),

time: 3180 us -> 567 us (0.18)
  waiting for transfers between devices: 2100 us -> 182 us
  matrix products: 567 us -> 10.4 us
  local copies, waits for them, and re-layouts: 247 us -> 52.7 us
  other arithmetic: 233 us -> 49.7 us
  Pallas kernels: 0 us -> 157 us
  starting transfers between devices: 8.99 us -> 103 us
    reduce_scatter x13 -> x0, waiting for transfers between devices: 987 us -> none  [the longest x4 286 us: frame_backward(): lax.psum_scatter(keys_term, 'dp', scatter_dimension=0, tiled=True)]
    all_gather x16 -> x0, waiting for transfers between devices: 584 us -> none  [the longest x8 289 us: frame_forward(): lax.all_gather(parts[:, 2], 'dp', axis=0, tiled=True)]
    psum x23 -> x0, waiting for transfers between devices: 442 us -> none  [head_total(): return lax.psum(partial_sum, 'tensor')]
    dot_general x53 -> x0, matrix products: 352 us -> none  [the longest x20 140 us: across_rows(): lax.dot_general(left, right, (((0,), (0,)), ((), ())), preferred_element_...]
    pallas_call x0 -> x11, Pallas kernels: none -> 157 us  [the longest x1 56.9 us: local_call(): pl.pallas_call(local_kernel, grid=(N // F,), in_specs=[pl.BlockSpec((F, D...]
    ppermute x3 -> x68, waiting for transfers between devices: 78.1 us -> 182 us  [the longest x52 98.6 us: linked(): return lax.ppermute(a, ('section', 'dp', 'tensor'), pairs)]
    ppermute x3 -> x68, starting transfers between devices: 6.82 us -> 103 us  [the longest x52 78 us: linked(): return lax.ppermute(a, ('section', 'dp', 'tensor'), pairs)]
    dot_general x28 -> x3, matrix products: 99.7 us -> 4.52 us  [matmul(): return jnp.dot(left, right, preferred_element_type=jnp.float32)]
  transfers between devices with their start and end apart: 56 -> 68, of which waited for: 53 -> 17; matrix products, arithmetic and copies ran while one was open for 15% -> 16% of each run, Pallas kernels for 0% -> 18%
where the time goes in v1:
time: 567 us; the launch traced here: 557 us
  waiting for transfers between devices  182 us (32%)
  Pallas kernels  157 us (28%)
  starting transfers between devices  103 us (18%)
  local copies, waits for them, and re-layouts  52.7 us (9%)
  other arithmetic  49.7 us (9%)
  matrix products  10.4 us (2%)
    ppermute x52, waiting for transfers between devices, linked(): return lax.ppermute(a, ('section', 'dp', 'tensor'), pairs)  98.6 us
    ppermute x52, starting transfers between devices, linked(): return lax.ppermute(a, ('section', 'dp', 'tensor'), pairs)  78 us
    ppermute x12, waiting for transfers between devices, swap(): return lax.ppermute(a, 'dp', [(i, i ^ 1 << bit) for i in range(count)])  69.6 us
    pallas_call x1, Pallas kernels, local_call(): pl.pallas_call(local_kernel, grid=(N // F,), in_specs=[pl.BlockSpec((F, D...  56.9 us
    pallas_call x2, Pallas kernels, weight_call(): pl.pallas_call(functools.partial(weight_kernel, plane_first=plane_first),...  27.3 us
    unnamed x123, local copies, waits for them, and re-layouts  18.1 us
    pallas_call x1, Pallas kernels, prepare_call(): pl.pallas_call(prepare_kernel, grid_spec=pltpu.PrefetchScalarGridSpec(num...  17.1 us
    ppermute x12, starting transfers between devices, swap(): return lax.ppermute(a, 'dp', [(i, i ^ 1 << bit) for i in range(count)])  16.5 us
  transfers between devices with their start and end apart: 68, of which 17 were waited for; matrix products, arithmetic and copies ran while one was open for 16% of the time, Pallas kernels for 18%

profile of v1, /device:TPU:3, one launch (start us, length us, event | category | flops | bytes accessed | tf_op | source)
XLA Modules:
  0.0 557.4 jit_solution(537635940267007897)
XLA Ops:
  56.3 4.9 collective-permute-start.17
  64.0 6.0 %global_forward.1 = (f32[256,1024]{1,0:T(8,128)}, bf16[256,1024]{1,0:T(8,128)(2,1)}, bf16[256,2048]{1,0:T(8,128)(2,1)}, bf16[256,2048]{1,0:T(8,128)(2,1)}, bf16[...) custom-call(s32[3]{0:T(128)} %pad_add_fusion.2.at_ref, bf16[256,1024]{1,0:T(8,128)(2,1)} %bitcast.201, ...), custom_call_target="tpu_custom_call" | custom-call | flops 16499999744 | bytes 15000000 | tf_op jit(solution)/shard_map/global_forward/pallas_call | solution.py:654
  71.3 15.9 %collective-permute-done.17 = bf16[1,3,64,1024]{3,2,1,0:T(8,128)(2,1)S(1)} collective-permute-done((bf16[1,3,64,1024]{3,2,1,0:T(8,128)(2,1)}, bf16[1,3,64,1024]{3,2,1,0:T(8,128)(2,1)S(1)}, u32[]{:S(2)}, u32[]{:S(2)}) %collective-permute-start.17) | collective-permute-done | bytes 393248 | tf_op jit(solution)/shard_map/ppermute | solution.py:1043
  88.6 17.1 %local_prepare.1 = (bf16[3,256,1024]{2,1,0:T(8,128)(2,1)}, bf16[3,256,2048]{2,1,0:T(8,128)(2,1)}, bf16[3,256,2048]{2,1,0:T(8,128)(2,1)}) custom-call(s32[3]{0:T(128)} %pad_add_fusion.2.at_ref, s32[3,256,1]{2,1,0:T(8,128)} %broadcast_in_dim_reshape.12.code_ref, bf16[768,1024]{1,0:T(8,128)(2,1)} %bitcast.206, bf16[2048,1024]{1,0:T(8,128)(2,1)} %bitcast.235, ...), custom_call_target="tpu_custom_call" | custom-call | flops 5500000256 | bytes 5000000 | tf_op jit(solution)/shard_map/local_prepare/pallas_call | solution.py:988
  105.7 13.9 %collective-permute-done.12.g_ref = bf16[256,1024]{1,0:T(8,128)(2,1)S(1)} collective-permute-done((bf16[256,1024]{1,0:T(8,128)(2,1)}, bf16[256,1024]{1,0:T(8,128)(2,1)S(1)}, u32[]{:S(2)}, u32[]{:S(2)}) %collective-permute-start.12) | collective-permute-done | bytes 524320 | tf_op jit(solution)/shard_map/ppermute | solution.py:1055
  120.4 56.9 %local_layer.1 = (bf16[3,256,1024]{2,1,0:T(8,128)(2,1)}, bf16[3,256,512]{2,1,0:T(8,128)(2,1)}, bf16[3,256,512]{2,1,0:T(8,128)(2,1)}, f32[3,256,1024]{2,1,0:T(8,1...) custom-call(bf16[256,1024]{1,0:T(8,128)(2,1)} %copy-done.36, ...), custom_call_target="tpu_custom_call" | custom-call | flops 62699999232 | bytes 57000000 | tf_op jit(solution)/shard_map/local_layer/pallas_call | solution.py:478
  188.1 14.8 %local_output.1 = bf16[4,3,64,1024]{3,2,1,0:T(8,128)(2,1)} custom-call(s32[3]{0:T(128)} %pad_add_fusion.2.at_ref, f32[768,1024]{1,0:T(8,128)} %bitcast.244, bf16[768,2048]{1,0:T(8,128)(2,1)} %bitcast.242, bf16[768,2048]{1,0:T(8,128)(2,1)} %bitcast.240, bf16[2048,1024]{1,0:T(8,128)(2,1)} %bitcast.236, bf16[2048,1024]{1,0:T(8,128)(2,1)} %collective-permute-done.11.dx_ref), custom_call_target="tpu_custom_call" | custom-call | flops 7699999744 | bytes 7000000 | tf_op jit(solution)/shard_map/local_output/pallas_call | solution.py:898
  203.8 6.0 %table_gradient.1 = (bf16[2,4,3,64,512]{4,3,2,1,0:T(8,128)(2,1)}, bf16[2,4,3,64,512]{4,3,2,1,0:T(8,128)(2,1)}) custom-call(s32[3]{0:T(128)} %pad_add_fusion.2.at_ref, s32[3,1,256]{2,1,0:T(1,128)} %broadcast_in_dim_reshape.10.code_ref, s32[3,1,256]{2,1,0:T(1,128)} %broadcast_in_dim.17.code_in_ref, bf16[3,256,512]{2,1,0:T(8,128)(2,1)} %get-tuple-element.218.own_ref, ...), custom_call_target="tpu_custom_call" | custom-call | flops 4400000000 | bytes 4000000 | tf_op jit(solution)/shard_map/table_gradient/pallas_call | solution.py:940
  212.5 4.9 global_backward.1
  223.4 14.0 %down_gradient.1 = (bf16[2,2,128,2048]{3,2,1,0:T(8,128)(2,1)}, bf16[2,2,128,2048]{3,2,1,0:T(8,128)(2,1)}) custom-call(s32[3]{0:T(128)} %pad_add_fusion.2.at_ref, bf16[256,1024]{1,0:T(8,128)(2,1)} %collective-permute-done.22.g_ref.gl, bf16[256,1024]{1,0:T(8,128)(2,1)} %collective-permute-done.23.gli, bf16[256,2048]{1,0:T(8,128)(2,1)} %get-tuple-element.119.gr, ...), custom_call_target="tpu_custom_call" | custom-call | flops 11000000512 | bytes 10000000 | tf_op jit(solution)/shard_map/down_gradient/pallas_call | solution.py:797
  241.7 13.4 %up_gradient.1 = (bf16[4,128,2048]{2,1,0:T(8,128)(2,1)}, bf16[4,128,2048]{2,1,0:T(8,128)(2,1)}) custom-call(s32[3]{0:T(128)} %pad_add_fusion.2.at_ref, bf16[256,1024]{1,0:T(8,128)(2,1)} %get-tuple-element.116.gl, bf16[256,1024]{1,0:T(8,128)(2,1)} %collective-permute-done.24.gli, bf16[256,2048]{1,0:T(8,128)(2,1)} %get-tuple-element.117.gr, ...), custom_call_target="tpu_custom_call" | custom-call | flops 11000000512 | bytes 10000000 | tf_op jit(solution)/shard_map/up_gradient/pallas_call | solution.py:797
  262.2 5.0 frame_attention_back.1
  286.9 48.4 %collective-permute-done.43 = bf16[1,3,64,1024]{3,2,1,0:T(8,128)(2,1)S(1)} collective-permute-done((bf16[1,3,64,1024]{3,2,1,0:T(8,128)(2,1)S(1)}, bf16[1,3,64,1024]{3,2,1,0:T(8,128)(2,1)S(1)}, u32[]{:S(2)}, u32[]{:S(2)}) %collective-permute-start.43) | collective-permute-done | bytes 393248 | tf_op jit(solution)/shard_map/ppermute | solution.py:1043
  347.7 6.1 %collective-permute-done.44 = bf16[1,3,64,1024]{3,2,1,0:T(8,128)(2,1)S(1)} collective-permute-done((bf16[1,3,64,1024]{3,2,1,0:T(8,128)(2,1)}, bf16[1,3,64,1024]{3,2,1,0:T(8,128)(2,1)S(1)}, u32[]{:S(2)}, u32[]{:S(2)}) %collective-permute-start.44) | collective-permute-done | bytes 393248 | tf_op jit(solution)/shard_map/ppermute | solution.py:1043
  360.3 14.2 %rest_gradient.1 = (bf16[4,128,2048]{2,1,0:T(8,128)(2,1)}, bf16[4,128,2048]{2,1,0:T(8,128)(2,1)}) custom-call(s32[3]{0:T(128)} %pad_add_fusion.2.at_ref, bf16[1024,1024]{1,0:T(8,128)(2,1)} %copy-done.17, bf16[1024,1024]{1,0:T(8,128)(2,1)} %copy-done.8, bf16[1024,256]{1,0:T(8,128)(2,1)} %frame_attention.1.ga, bf16[1024,256]{1,0:T(8,128)(2,1)} %get-tuple-element.131.gq, ...), custom_call_target="tpu_custom_call" | custom-call | flops 11000000 | bytes 10000 | tf_op jit(solution)/shard_map/rest_gradient/pallas_call | solution.py:848
  380.2 8.7 %collective-permute-start.51 = (bf16[1,64,1024]{2,1,0:T(8,128)(2,1)S(1)}, bf16[1,64,1024]{2,1,0:T(8,128)(2,1)S(1)}, u32[]{:S(2)}, u32[]{:S(2)}) collective-permute-start(bf16[1,64,1024]{2,1,0:T(8,128)(2,1)S(1)} %get-tuple-element.225), channel_id=1, source_target_pairs={{0,4},{1,5},{2,6},{3,7},{4,0},{5,1},{6,2},{7,3},{8,12},{9,13},{10,... | collective-permute-start | bytes 393224 | tf_op jit(solution)/shard_map/ppermute | solution.py:1043
  398.8 18.7 %collective-permute-done.52 = bf16[1,64,1024]{2,1,0:T(8,128)(2,1)S(1)} collective-permute-done((bf16[1,64,1024]{2,1,0:T(8,128)(2,1)S(1)}, bf16[1,64,1024]{2,1,0:T(8,128)(2,1)S(1)}, u32[]{:S(2)}, u32[]{:S(2)}) %collective-permute-start.52) | collective-permute-done | bytes 131104 | tf_op jit(solution)/shard_map/ppermute | solution.py:1043
  430.4 8.5 %collective-permute-start.56 = (bf16[2,128,2048]{2,1,0:T(8,128)(2,1)}, bf16[2,128,2048]{2,1,0:T(8,128)(2,1)}, u32[]{:S(2)}, u32[]{:S(2)}) collective-permute-start(bf16[2,128,2048]{2,1,0:T(8,128)(2,1)} %slice.254), channel_id=1, source_target_pairs={{0,4},{2,6},{4,0},{6,2},{8,12},{10,14},{12,8},{14,10},{1,5},{3,7},... | collective-permute-start | bytes 3145736 | tf_op jit(solution)/shard_map/ppermute | solution.py:1144
  452.4 19.6 %collective-permute-done.57 = bf16[128,2048]{1,0:T(8,128)(2,1)} collective-permute-done((bf16[128,2048]{1,0:T(8,128)(2,1)}, bf16[128,2048]{1,0:T(8,128)(2,1)}, u32[]{:S(2)}, u32[]{:S(2)}) %collective-permute-start.57) | collective-permute-done | bytes 524320 | tf_op jit(solution)/shard_map/ppermute | solution.py:1144
  472.0 10.0 %collective-permute-done.59 = bf16[4,208,512]{2,1,0:T(8,128)(2,1)} collective-permute-done((bf16[4,208,512]{2,1,0:T(8,128)(2,1)}, bf16[4,208,512]{2,1,0:T(8,128)(2,1)}, u32[]{:S(2)}, u32[]{:S(2)}) %collective-permute-start.59) | collective-permute-done | bytes 852000 | tf_op jit(solution)/shard_map/ppermute | solution.py:1144
  494.8 5.0 collective-permute-done.65
  500.7 24.3 %collective-permute-done.64 = bf16[128,2048]{1,0:T(8,128)(2,1)S(1)} collective-permute-done((bf16[128,2048]{1,0:T(8,128)(2,1)S(1)}, bf16[128,2048]{1,0:T(8,128)(2,1)S(1)}, u32[]{:S(2)}, u32[]{:S(2)}) %collective-permute-start.64) | collective-permute-done | bytes 524320 | tf_op jit(solution)/shard_map/ppermute | solution.py:1144
  526.1 10.1 %collective-permute-done.63 = bf16[128,2048]{1,0:T(8,128)(2,1)S(1)} collective-permute-done((bf16[128,2048]{1,0:T(8,128)(2,1)S(1)}, bf16[128,2048]{1,0:T(8,128)(2,1)S(1)}, u32[]{:S(2)}, u32[]{:S(2)}) %collective-permute-start.63) | collective-permute-done | bytes 524320 | tf_op jit(solution)/shard_map/ppermute | solution.py:1144
  543.5 5.3 collective-permute-start.67
  (378 shorter events, 203.4 us)
Async XLA Ops:
  12.1 49.1 %collective-permute-start.10 = (bf16[1024,2048]{1,0:T(8,128)(2,1)}, bf16[1024,2048]{1,0:T(8,128)(2,1)}, u32[]{:S(2)}, u32[]{:S(2)}) collective-permute-start(bf16[1024,2048]{1,0:T(8,128)(2,1)} %bitcast.229), channel_id=1, source_target_pairs={{0,1},{1,0},{2,3},{3,2},{4,5},{5,4},{6,7},{7,6},{8,9},{9,8},{10,11... | collective-permute-start | bytes 12582920 | tf_op jit(solution)/shard_map/ppermute | solution.py:1043
  12.5 51.4 %collective-permute-start.11 = (bf16[2048,1024]{1,0:T(8,128)(2,1)}, bf16[2048,1024]{1,0:T(8,128)(2,1)}, u32[]{:S(2)}, u32[]{:S(2)}) collective-permute-start(bf16[2048,1024]{1,0:T(8,128)(2,1)} %bitcast.233), channel_id=1, source_target_pairs={{0,1},{1,0},{2,3},{3,2},{4,5},{5,4},{6,7},{7,6},{8,9},{9,8},{10,11... | collective-permute-start | bytes 12582920 | tf_op jit(solution)/shard_map/ppermute | solution.py:1043
  13.2 43.0 %collective-permute-start.9 = (bf16[512,1024]{1,0:T(8,128)(2,1)}, bf16[512,1024]{1,0:T(8,128)(2,1)}, u32[]{:S(2)}, u32[]{:S(2)}) collective-permute-start(bf16[512,1024]{1,0:T(8,128)(2,1)} %bitcast.18.oo_ref.woo), channel_id=1, source_target_pairs={{0,1},{1,0},{2,3},{3,2},{4,5},{5,4},{6,7},{7,6},{8,9},{9,8},{10,11... | collective-permute-start | bytes 3145736 | tf_op jit(solution)/shard_map/ppermute | solution.py:1043
  38.7 67.0 %collective-permute-start.19 = (bf16[3,1024,512]{2,1,0:T(8,128)(2,1)}, bf16[3,1024,512]{2,1,0:T(8,128)(2,1)}, u32[]{:S(2)}, u32[]{:S(2)}) collective-permute-start(bf16[3,1024,512]{2,1,0:T(8,128)(2,1)} %bitcast.211), channel_id=1, source_target_pairs={{0,1},{1,0},{2,3},{3,2},{4,5},{5,4},{6,7},{7,6},{8,9},{9,8},{10,11... | collective-permute-start | bytes 9437192 | tf_op jit(solution)/shard_map/ppermute | solution.py:1043
  69.9 49.6 %collective-permute-start.12 = (bf16[256,1024]{1,0:T(8,128)(2,1)}, bf16[256,1024]{1,0:T(8,128)(2,1)S(1)}, u32[]{:S(2)}, u32[]{:S(2)}) collective-permute-start(bf16[256,1024]{1,0:T(8,128)(2,1)} %get-tuple-element.95), channel_id=1, source_target_pairs={{0,16},{1,17},{2,18},{3,19},{4,20},{5,21},{6,22},{7,23},{8,24},{9,... | collective-permute-start | bytes 1572872 | tf_op jit(solution)/shard_map/ppermute | solution.py:1055
  181.7 37.4 %collective-permute-start.27 = (bf16[768,2048]{1,0:T(8,128)(2,1)}, bf16[768,2048]{1,0:T(8,128)(2,1)}, u32[]{:S(2)}, u32[]{:S(2)}) collective-permute-start(bf16[768,2048]{1,0:T(8,128)(2,1)} %bitcast.239), channel_id=1, source_target_pairs={{0,1},{1,0},{2,3},{3,2},{4,5},{5,4},{6,7},{7,6},{8,9},{9,8},{10,11... | collective-permute-start | bytes 9437192 | tf_op jit(solution)/shard_map/ppermute | solution.py:1043
  187.4 53.6 %collective-permute-start.30 = (bf16[768,2048]{1,0:T(8,128)(2,1)}, bf16[768,2048]{1,0:T(8,128)(2,1)}, u32[]{:S(2)}, u32[]{:S(2)}) collective-permute-start(bf16[768,2048]{1,0:T(8,128)(2,1)} %bitcast.238), channel_id=1, source_target_pairs={{0,1},{1,0},{2,3},{3,2},{4,5},{5,4},{6,7},{7,6},{8,9},{9,8},{10,11... | collective-permute-start | bytes 9437192 | tf_op jit(solution)/shard_map/ppermute | solution.py:1043
  219.1 50.7 %collective-permute-start.45 = (bf16[1,64,1024]{2,1,0:T(8,128)(2,1)}, bf16[1,64,1024]{2,1,0:T(8,128)(2,1)S(1)}, u32[]{:S(2)}, u32[]{:S(2)}) collective-permute-start(bf16[1,64,1024]{2,1,0:T(8,128)(2,1)} %get-tuple-element.228), channel_id=1, source_target_pairs={{0,4},{1,5},{2,6},{3,7},{4,0},{5,1},{6,2},{7,3},{8,12},{9,13},{10,... | collective-permute-start | bytes 393224 | tf_op jit(solution)/shard_map/ppermute | solution.py:1043
  238.2 39.5 %collective-permute-start.47 = (bf16[1,64,1024]{2,1,0:T(8,128)(2,1)}, bf16[1,64,1024]{2,1,0:T(8,128)(2,1)}, u32[]{:S(2)}, u32[]{:S(2)}) collective-permute-start(bf16[1,64,1024]{2,1,0:T(8,128)(2,1)} %get-tuple-element.226), channel_id=1, source_target_pairs={{0,12},{1,13},{2,14},{3,15},{4,8},{5,9},{6,10},{7,11},{8,4},{9,5},... | collective-permute-start | bytes 393224 | tf_op jit(solution)/shard_map/ppermute | solution.py:1043
  269.8 90.5 %collective-permute-start.37 = (bf16[3,3,256,512]{3,2,1,0:T(8,128)(2,1)}, bf16[3,3,256,512]{3,2,1,0:T(8,128)(2,1)}, u32[]{:S(2)}, u32[]{:S(2)}) collective-permute-start(bf16[3,3,256,512]{3,2,1,0:T(8,128)(2,1)} %get-tuple-element.139), channel_id=1, source_target_pairs={{0,1},{1,0},{2,3},{3,2},{4,5},{5,4},{6,7},{7,6},{8,9},{9,8},{10,11... | collective-permute-start | bytes 7077896 | tf_op jit(solution)/shard_map/ppermute | solution.py:1043
  277.7 61.4 %collective-permute-start.40 = (bf16[512,1024]{1,0:T(8,128)(2,1)}, bf16[512,1024]{1,0:T(8,128)(2,1)S(1)}, u32[]{:S(2)}, u32[]{:S(2)}) collective-permute-start(bf16[512,1024]{1,0:T(8,128)(2,1)} %slice.332), channel_id=1, source_target_pairs={{0,1},{1,0},{2,3},{3,2},{4,5},{5,4},{6,7},{7,6},{8,9},{9,8},{10,11... | collective-permute-start | bytes 3145736 | tf_op jit(solution)/shard_map/ppermute | solution.py:1043
  278.4 96.2 %collective-permute-start.39 = (bf16[4,128,2048]{2,1,0:T(8,128)(2,1)}, bf16[4,128,2048]{2,1,0:T(8,128)(2,1)}, u32[]{:S(2)}, u32[]{:S(2)}) collective-permute-start(bf16[4,128,2048]{2,1,0:T(8,128)(2,1)} %get-tuple-element.142), channel_id=1, source_target_pairs={{0,2},{2,0},{4,6},{6,4},{8,10},{10,8},{12,14},{14,12},{1,3},{3,1},... | collective-permute-start | bytes 6291464 | tf_op jit(solution)/shard_map/ppermute | solution.py:1144
  279.6 94.9 %collective-permute-start.38 = (bf16[2,2,128,2048]{3,2,1,0:T(8,128)(2,1)}, bf16[2,2,128,2048]{3,2,1,0:T(8,128)(2,1)}, u32[]{:S(2)}, u32[]{:S(2)}) collective-permute-start(bf16[2,2,128,2048]{3,2,1,0:T(8,128)(2,1)} %get-tuple-element.141), channel_id=1, source_target_pairs={{0,4},{2,6},{4,0},{6,2},{8,12},{10,14},{12,8},{14,10},{1,5},{3,7},... | collective-permute-start | bytes 6291464 | tf_op jit(solution)/shard_map/ppermute | solution.py:1144
  283.4 51.9 %collective-permute-start.43 = (bf16[1,3,64,1024]{3,2,1,0:T(8,128)(2,1)S(1)}, bf16[1,3,64,1024]{3,2,1,0:T(8,128)(2,1)S(1)}, u32[]{:S(2)}, u32[]{:S(2)}) collective-permute-start(bf16[1,3,64,1024]{3,2,1,0:T(8,128)(2,1)S(1)} %copy-done.43), channel_id=1, source_target_pairs={{16,24},{17,25},{18,26},{19,27},{20,28},{21,29},{22,30},{23,31},{2... | collective-permute-start | bytes 1179656 | tf_op jit(solution)/shard_map/ppermute | solution.py:1043
  357.6 66.6 %collective-permute-start.54 = (bf16[2,4,3,64,512]{4,3,2,1,0:T(8,128)(2,1)}, bf16[2,4,3,64,512]{4,3,2,1,0:T(8,128)(2,1)}, u32[]{:S(2)}, u32[]{:S(2)}) collective-permute-start(bf16[2,4,3,64,512]{4,3,2,1,0:T(8,128)(2,1)} %get-tuple-element.153), channel_id=1, source_target_pairs={{16,0},{17,1},{18,2},{19,3},{20,4},{21,5},{22,6},{23,7},{24,8},{25... | collective-permute-start | bytes 4718600 | tf_op jit(solution)/shard_map/ppermute | solution.py:1058
  377.2 47.5 %collective-permute-start.49 = (bf16[4,128,2048]{2,1,0:T(8,128)(2,1)}, bf16[4,128,2048]{2,1,0:T(8,128)(2,1)}, u32[]{:S(2)}, u32[]{:S(2)}) collective-permute-start(bf16[4,128,2048]{2,1,0:T(8,128)(2,1)} %get-tuple-element.146), channel_id=1, source_target_pairs={{0,2},{2,0},{4,6},{6,4},{8,10},{10,8},{12,14},{14,12},{1,3},{3,1},... | collective-permute-start | bytes 6291464 | tf_op jit(solution)/shard_map/ppermute | solution.py:1144
  417.5 34.9 %collective-permute-start.60 = (bf16[4,3,64,1024]{3,2,1,0:T(8,128)(2,1)}, bf16[4,3,64,1024]{3,2,1,0:T(8,128)(2,1)}, u32[]{:S(2)}, u32[]{:S(2)}) collective-permute-start(bf16[4,3,64,1024]{3,2,1,0:T(8,128)(2,1)} %copy-done.11), channel_id=1, source_target_pairs={{16,0},{17,1},{18,2},{19,3},{20,4},{21,5},{22,6},{23,7},{24,8},{25... | collective-permute-start | bytes 4718600 | tf_op jit(solution)/shard_map/ppermute | solution.py:1058
  430.4 51.6 %collective-permute-start.56 = (bf16[2,128,2048]{2,1,0:T(8,128)(2,1)}, bf16[2,128,2048]{2,1,0:T(8,128)(2,1)}, u32[]{:S(2)}, u32[]{:S(2)}) collective-permute-start(bf16[2,128,2048]{2,1,0:T(8,128)(2,1)} %slice.254), channel_id=1, source_target_pairs={{0,4},{2,6},{4,0},{6,2},{8,12},{10,14},{12,8},{14,10},{1,5},{3,7},... | collective-permute-start | bytes 3145736 | tf_op jit(solution)/shard_map/ppermute | solution.py:1144
  439.9 42.1 %collective-permute-start.58 = (bf16[2,128,2048]{2,1,0:T(8,128)(2,1)}, bf16[2,128,2048]{2,1,0:T(8,128)(2,1)}, u32[]{:S(2)}, u32[]{:S(2)}) collective-permute-start(bf16[2,128,2048]{2,1,0:T(8,128)(2,1)} %slice_bitcast_fusion), channel_id=1, source_target_pairs={{0,2},{2,0},{4,6},{6,4},{8,10},{10,8},{12,14},{14,12},{1,3},{3,1},... | collective-permute-start | bytes 3145736 | tf_op jit(solution)/shard_map/ppermute | solution.py:1144
  445.3 36.7 %collective-permute-start.59 = (bf16[4,208,512]{2,1,0:T(8,128)(2,1)}, bf16[4,208,512]{2,1,0:T(8,128)(2,1)}, u32[]{:S(2)}, u32[]{:S(2)}) collective-permute-start(bf16[4,208,512]{2,1,0:T(8,128)(2,1)} %slice_bitcast_fusion.2), channel_id=1, source_target_pairs={{0,2},{2,0},{4,6},{6,4},{8,10},{10,8},{12,14},{14,12},{1,3},{3,1},... | collective-permute-start | bytes 2555912 | tf_op jit(solution)/shard_map/ppermute | solution.py:1144
  485.6 39.5 %collective-permute-start.64 = (bf16[128,2048]{1,0:T(8,128)(2,1)S(1)}, bf16[128,2048]{1,0:T(8,128)(2,1)S(1)}, u32[]{:S(2)}, u32[]{:S(2)}) collective-permute-start(bf16[128,2048]{1,0:T(8,128)(2,1)S(1)} %slice_bitcast_fusion.3), channel_id=1, source_target_pairs={{0,8},{2,10},{4,12},{6,14},{8,0},{10,2},{12,4},{14,6},{1,9},{3,11}... | collective-permute-start | bytes 1572872 | tf_op jit(solution)/shard_map/ppermute | solution.py:1144
  491.4 44.9 %collective-permute-start.63 = (bf16[128,2048]{1,0:T(8,128)(2,1)S(1)}, bf16[128,2048]{1,0:T(8,128)(2,1)S(1)}, u32[]{:S(2)}, u32[]{:S(2)}) collective-permute-start(bf16[128,2048]{1,0:T(8,128)(2,1)S(1)} %slice_bitcast_fusion.6), channel_id=1, source_target_pairs={{0,8},{2,10},{4,12},{6,14},{8,0},{10,2},{12,4},{14,6},{1,9},{3,11}... | collective-permute-start | bytes 1572872 | tf_op jit(solution)/shard_map/ppermute | solution.py:1144
  492.1 60.2 %collective-permute-start.61 = (bf16[4,3,64,1024]{3,2,1,0:T(8,128)(2,1)S(1)}, bf16[4,3,64,1024]{3,2,1,0:T(8,128)(2,1)}, u32[]{:S(2)}, u32[]{:S(2)}) collective-permute-start(bf16[4,3,64,1024]{3,2,1,0:T(8,128)(2,1)S(1)} %broadcast_select_fusion.1), channel_id=1, source_target_pairs={{0,1},{1,0},{2,3},{3,2},{4,5},{5,4},{6,7},{7,6},{8,9},{9,8},{10,11... | collective-permute-start | bytes 4718600 | tf_op jit(solution)/shard_map/ppermute | solution.py:1043
  500.7 41.7 %collective-permute-start.66 = (bf16[208,512]{1,0:T(8,128)(2,1)}, bf16[208,512]{1,0:T(8,128)(2,1)}, u32[]{:S(2)}, u32[]{:S(2)}) collective-permute-start(bf16[208,512]{1,0:T(8,128)(2,1)} %slice_bitcast_fusion.19), channel_id=1, source_target_pairs={{0,8},{2,10},{4,12},{6,14},{8,0},{10,2},{12,4},{14,6},{1,9},{3,11}... | collective-permute-start | bytes 638984 | tf_op jit(solution)/shard_map/ppermute | solution.py:1144
  (101 other events, 1114.8 us)
